TPU v7x, 32 devices: a whole 2x2x4 slice. The times are simulated.
32 devices in a mesh: req: 8 (over y, x, core), rep: 4 (over z).
Axes of the slice: x: 2, y: 2, z: 4, core: 2. Of those that a mesh axis runs over, the one named last changes fastest.
Arguments:
- tokens: bfloat16 [32, 2, 2048], P('req'), may hold values from -6 to 6
- norm_gains: float32 [2, 2048], replicated, may hold values from 0.1 to 1.9
- w_kv: bfloat16 [2048, 2, 2048], P(None, None, 'rep'), may hold values from -0.125 to 0.125
- w_query: bfloat16 [8, 2048, 2048], P('req', None, 'rep'), may hold values from -0.125 to 0.125
- w_out: bfloat16 [8, 2048, 2048], P('req', 'rep'), may hold values from -0.5 to 0.5
- w_gate: bfloat16 [8, 2048, 5632], P('req', None, 'rep'), may hold values from -0.125 to 0.125
- w_up: bfloat16 [8, 2048, 5632], P('req', None, 'rep'), may hold values from -0.125 to 0.125
- w_down: bfloat16 [8, 5632, 2048], P('req', 'rep'), may hold values from -0.078125 to 0.078125
- kv_pages: bfloat16 [2048, 16, 2, 2048], P('req', None, None, 'rep'), may hold values from -80 to 80
- page_table: int32 [32, 64], P('req'), may hold values from 0 to 255, as said below
- cache_len: int32 [32], P('req'), may hold values from 1 to 1024
- route_ids: int32 [32, 2, 2, 2], P('req'), may hold values from 0 to 7, all different within a row
- route_gates: bfloat16 [32, 2, 2, 2], P('req'), may hold values from 0.19921875 to 1
- new_slot: int32 [32], P('req'), may hold values from 0 to 31, each once
Outputs:
- layer_out: bfloat16 [32, 2, 2048], P('req')
Inputs may be any that keep to these rules, and one draw needn't show every extreme that they name: `page_table`: row i lists 64 distinct pages of the pool of the device that holds request i; two requests of one device share no page.
All inputs are finite; a program needn't handle non-finite values.
Results may differ from a plain program's by a relative error of at most 0.022.
Values may be sent and summed in bfloat16 or wider, within the bound.
A program may use at most 128 MiB of HBM per device.

v0:
```python
import math

import jax
import jax.numpy as jnp
from jax import lax
from jax.sharding import PartitionSpec as P

HD = 128
EXPERTS = 8


EPSILON = 1e-06
MASKED = -1e30


def normalize(values, gain_row):
    scaling = lax.rsqrt(jnp.mean(values * values, axis=-1, keepdims=True) + EPSILON)
    return (values * scaling * gain_row).astype(jnp.bfloat16)


def expert_share(ids_block, gates_block, expert):
    return jnp.sum(jnp.where(ids_block == expert, gates_block.astype(jnp.float32), 0.0), axis=-1)


def attend(queries, cache_keys, cache_values, lengths, extra_keys, extra_values, extra_live):
    inv_scale = 1.0 / math.sqrt(queries.shape[-1])
    cache_scores = (
        jnp.einsum("jskhc,jlhc->jskhl", queries, cache_keys, preferred_element_type=jnp.float32)
        * inv_scale
    )
    alive_mask = jnp.arange(cache_keys.shape[1], dtype=jnp.int32)[None, :] < lengths[:, None]
    cache_scores = jnp.where(alive_mask[:, None, None, None, :], cache_scores, MASKED)
    extra_scores = (
        jnp.einsum("jskhc,jxhc->jskhx", queries, extra_keys, preferred_element_type=jnp.float32)
        * inv_scale
    )
    extra_scores = jnp.where(extra_live[None, :, None, None, :], extra_scores, MASKED)
    highest = jnp.maximum(jnp.max(cache_scores, axis=-1), jnp.max(extra_scores, axis=-1))[..., None]
    cache_exp = jnp.exp(cache_scores - highest)
    extra_exp = jnp.exp(extra_scores - highest)
    denominator = (jnp.sum(cache_exp, axis=-1) + jnp.sum(extra_exp, axis=-1))[..., None]
    cache_weight = (cache_exp / denominator).astype(jnp.bfloat16)
    extra_weight = (extra_exp / denominator).astype(jnp.bfloat16)
    mixture = jnp.einsum(
        "jskhl,jlhc->jskhc", cache_weight, cache_values, preferred_element_type=jnp.float32
    )
    mixture = mixture + jnp.einsum(
        "jskhx,jxhc->jskhc", extra_weight, extra_values, preferred_element_type=jnp.float32
    )
    return mixture.astype(jnp.bfloat16)


def combine(term_fn, all_rows):
    partial_value = lax.psum_scatter(
        term_fn(jnp.int32(0), all_rows // lax.axis_size("req") * lax.axis_size("req")).astype(
            jnp.bfloat16
        ),
        "req",
        scatter_dimension=0,
        tiled=True,
    )
    return lax.psum(partial_value, "rep").astype(jnp.float32)


def shards(
    tokens,
    norm_gains,
    w_kv,
    w_query,
    w_out,
    w_gate,
    w_up,
    w_down,
    kv_pages,
    page_table,
    cache_len,
    route_ids,
    route_gates,
    new_slot,
):
    rows_dev = tokens.shape[0]
    req_count = lax.axis_size("req")
    all_rows = rows_dev * req_count
    holders = req_count // EXPERTS
    expert = lax.axis_index("req") // holders
    head_dim = HD
    heads_rep = kv_pages.shape[-1] // head_dim
    heads_dev = w_query.shape[-1] // head_dim
    inputs = tokens.astype(jnp.float32)
    normed = normalize(inputs, norm_gains[0])
    cache_pages = kv_pages[page_table].reshape(rows_dev, -1, 2, heads_rep, head_dim)
    cache_keys = cache_pages[:, :, 0]
    cache_values = cache_pages[:, :, 1]
    experts_row = jnp.arange(EXPERTS, dtype=jnp.int32)

    def fresh_kv(normed_rows):
        return jnp.einsum(
            "jd,dtc->jtc", normed_rows, w_kv, preferred_element_type=jnp.float32
        ).astype(jnp.bfloat16)

    def pair_kv(first_kv, second_kv):
        return jnp.stack([first_kv, second_kv], axis=1).reshape(rows_dev, 2, 2, heads_rep, head_dim)

    first_fresh = fresh_kv(normed[:, 0])

    def section(step_list, gathered, slot_map, all_ids, all_gates, extra_kv):
        step_count = len(step_list)
        first_step = step_list[0]
        step_span = slice(first_step, first_step + step_count)
        inverse = (
            jnp.zeros((all_rows,), jnp.int32)
            .at[slot_map]
            .set(jnp.arange(all_rows, dtype=jnp.int32))
        )
        queries = jnp.einsum(
            "bsd,dc->bsc", gathered, w_query[0], preferred_element_type=jnp.float32
        ).astype(jnp.bfloat16)
        columns = []
        own_ids = []
        for position, current in enumerate(step_list):
            if current == 0:
                columns.append(queries[:, position])
                own_ids.append(route_ids[:, 0, 0])
            else:
                columns.append(jnp.take(queries[:, position], slot_map, axis=0))
                own_ids.append(jnp.take(all_ids[:, 0, 1], new_slot, axis=0))
        ordered = jnp.stack(columns, axis=1).reshape(
            req_count, rows_dev, step_count, heads_dev * head_dim
        )
        arrived = lax.all_to_all(ordered, "req", split_axis=0, concat_axis=0, tiled=True)
        arrived = arrived.reshape(EXPERTS, holders, rows_dev, step_count, heads_dev, head_dim)
        chosen = (jnp.stack(own_ids, axis=1)[..., None] == experts_row).astype(jnp.bfloat16)
        picked = jnp.einsum(
            "jske,egjshc->jskghc", chosen, arrived, preferred_element_type=jnp.float32
        ).astype(jnp.bfloat16)
        picked = picked.reshape(rows_dev, step_count, 2, heads_rep, head_dim)
        extra_live = jnp.array(
            [[extra_slot <= current for extra_slot in range(2)] for current in step_list]
        )
        result = attend(
            picked,
            cache_keys,
            cache_values,
            cache_len,
            extra_kv[:, :, 0],
            extra_kv[:, :, 1],
            extra_live,
        )
        result = result.reshape(rows_dev, step_count, 2, holders, heads_dev, head_dim)
        spread = jnp.einsum(
            "jske,jskghc->egjshc", chosen, result, preferred_element_type=jnp.float32
        ).astype(jnp.bfloat16)
        returned = lax.all_to_all(
            spread.reshape(req_count, rows_dev, step_count, heads_dev * head_dim),
            "req",
            split_axis=0,
            concat_axis=0,
            tiled=True,
        )
        returned = returned.reshape(all_rows, step_count, heads_dev * head_dim)
        answers = jnp.stack(
            [
                (
                    returned[:, position]
                    if current == 0
                    else jnp.take(returned[:, position], inverse, axis=0)
                )
                for position, current in enumerate(step_list)
            ],
            axis=1,
        )
        attn_share = expert_share(all_ids[:, 0, step_span], all_gates[:, 0, step_span], expert)
        ffn_share = expert_share(all_ids[:, 1, step_span], all_gates[:, 1, step_span], expert)

        def attn_term(first_row, row_count):
            return (
                jnp.einsum("bsc,cd->bsd", answers, w_out[0], preferred_element_type=jnp.float32)
                * attn_share[..., None]
            )

        hidden = inputs[:, step_span] + combine(attn_term, all_rows)
        hidden_normed = normalize(hidden, norm_gains[1])
        block_rows = lax.all_gather(hidden_normed, "req", axis=0, tiled=True)
        gate_part = jnp.einsum(
            "bsd,df->bsf", block_rows, w_gate[0], preferred_element_type=jnp.float32
        )
        up_part = jnp.einsum("bsd,df->bsf", block_rows, w_up[0], preferred_element_type=jnp.float32)
        hidden_units = (jax.nn.silu(gate_part) * up_part).astype(jnp.bfloat16)

        def ffn_term(first_row, row_count):
            return (
                jnp.einsum(
                    "bsf,fd->bsd", hidden_units, w_down[0], preferred_element_type=jnp.float32
                )
                * ffn_share[..., None]
            )

        return (hidden + combine(ffn_term, all_rows)).astype(jnp.bfloat16)

    first_rows, all_ids, all_gates, slot_map = (
        lax.all_gather(normed[:, 0:1], "req", axis=0, tiled=True),
        lax.all_gather(route_ids, "req", axis=0, tiled=True),
        lax.all_gather(route_gates, "req", axis=0, tiled=True),
        lax.all_gather(new_slot, "req", axis=0, tiled=True),
    )
    early = section(
        (0,), first_rows, slot_map, all_ids, all_gates, pair_kv(first_fresh, first_fresh)
    )
    second_rows = lax.all_gather(normed[:, 1:2], "req", axis=0, tiled=True)
    second_fresh = fresh_kv(jnp.take(second_rows[:, 0], new_slot, axis=0))
    later = section(
        (1,), second_rows, slot_map, all_ids, all_gates, pair_kv(first_fresh, second_fresh)
    )
    return jnp.concatenate([early, later], axis=1)


def solution(mesh):
    in_specs = (
        P("req", None, None),
        P(),
        P(None, None, "rep"),
        P("req", None, "rep"),
        P("req", "rep", None),
        P("req", None, "rep"),
        P("req", None, "rep"),
        P("req", "rep", None),
        P("req", None, None, "rep"),
        P("req", None),
        P("req"),
        P("req", None, None, None),
        P("req", None, None, None),
        P("req"),
    )
    out_specs = P("req", None, None)
    return jax.shard_map(shards, mesh=mesh, in_specs=in_specs, out_specs=out_specs, check_vma=False)
```

profile of v0, /device:TPU:0, one launch (start us, length us, event | category | flops | bytes accessed | tf_op | source)
XLA Modules:
  0.0 354.0 jit_solution(17404225688148960483)
XLA Ops:
  9.2 10.8 %all_gather.21 = bf16[32,1,2048]{2,1,0:T(2,128)(2,1)S(1)} all-gather(bf16[4,1,2048]{2,1,0:T(2,128)(2,1)S(1)} %copy.189), channel_id=1, replica_groups=mesh['req'=8,'rep'=4] {'req'}, dimensions={0}, use_global_device_ids=true | all-gather | bytes 147456 | tf_op jit(solution)/shard_map/all_gather | solution.py:201
  20.0 2.0 fusion.64
  22.6 3.3 all-to-all-start
  27.4 1.4 fusion.182
  30.4 8.4 %all-reduce = s32[32]{0:T(128)S(1)} all-reduce(s32[32]{0:T(128)S(1)} %dynamic-update-slice), channel_id=1, replica_groups=mesh['req'=8,'rep'=4] {'req'}, use_global_device_ids=true, to_apply=%add | all-reduce | flops 32 | bytes 256
  41.7 25.4 %gather_fusion = bf16[256,16,2,512]{3,2,1,0:T(2,128)(2,1)} fusion(bf16[256,16,2,512]{3,2,1,0:T(2,128)(2,1)} %param.26, s32[1024]{0:T(1024)S(1)} %pad_clamp_fusion.3), kind=kCustom, calls=%fused_computation.2 | custom fusion | bytes 16778240 | tf_op jit(solution)/shard_map/gather | solution.py:91
  67.0 14.0 %reshape.554 = bf16[4,1024,2,4,128]{4,3,2,1,0:T(4,128)(2,1)} reshape(bf16[256,16,2,512]{3,2,1,0:T(2,128)(2,1)} %gather_fusion) | data formatting | bytes 16777216 | tf_op jit(solution)/shard_map/reshape | solution.py:91
  81.1 8.4 %fusion.179 = (bf16[4,1024,1,4,128]{4,3,2,1,0:T(4,128)(2,1)}, bf16[4,1024,1,4,128]{4,3,2,1,0:T(4,128)(2,1)}) fusion(bf16[4,1024,2,4,128]{4,3,2,1,0:T(4,128)(2,1)} %reshape.554), kind=kLoop, calls=%fused_computation.212 | loop fusion | bytes 16777216 | tf_op jit(solution)/shard_map/slice | solution.py:92
  90.3 8.4 %all_gather.23 = bf16[32,2,2,2]{3,2,1,0:T(2,128)(2,1)S(1)} all-gather(bf16[4,2,2,2]{3,2,1,0:T(2,128)(2,1)S(1)} %copy.205), channel_id=1, replica_groups=mesh['req'=8,'rep'=4] {'req'}, dimensions={0}, use_global_device_ids=true | all-gather | bytes 576 | tf_op jit(solution)/shard_map/all_gather | solution.py:203
  98.7 8.9 %all_gather.22 = s32[32,2,2,2]{3,2,1,0:T(2,128)S(1)} all-gather(s32[4,2,2,2]{3,2,1,0:T(2,128)S(1)} %copy.204), channel_id=1, replica_groups=mesh['req'=8,'rep'=4] {'req'}, dimensions={0}, use_global_device_ids=true | all-gather | bytes 1152 | tf_op jit(solution)/shard_map/all_gather | solution.py:202
  107.6 8.7 %all_gather.25 = bf16[32,1,2048]{2,1,0:T(2,128)(2,1)S(1)} all-gather(bf16[4,1,2048]{2,1,0:T(2,128)(2,1)S(1)} %copy.209), channel_id=1, replica_groups=mesh['req'=8,'rep'=4] {'req'}, dimensions={0}, use_global_device_ids=true | all-gather | bytes 147456 | tf_op jit(solution)/shard_map/all_gather | solution.py:209
  116.3 2.0 fusion.67
  119.7 2.9 fusion.77
  124.4 3.5 all-to-all-start.2
  128.1 3.5 fusion.183
  133.1 3.5 fusion.184
  137.7 3.1 fusion.13
  143.0 3.9 %all-to-all-start.3 = ((bf16[8,4,1,512]{3,1,2,0:T(4,128)(2,1)}), bf16[8,4,1,512]{3,1,2,0:T(4,128)(2,1)S(1)}, u32[]{:S(2)}, u32[]{:S(2)}) async-start(bf16[8,4,1,512]{3,1,2,0:T(4,128)(2,1)} %copy.223), calls=%async_computation.3 | async-start | bytes 65536 | tf_op jit(solution)/shard_map/all_to_all | solution.py:153
  147.9 3.9 %all-to-all-done.3 = bf16[8,4,1,512]{3,1,2,0:T(4,128)(2,1)S(1)} async-done(((bf16[8,4,1,512]{3,1,2,0:T(4,128)(2,1)}), bf16[8,4,1,512]{3,1,2,0:T(4,128)(2,1)S(1)}, u32[]{:S(2)}, u32[]{:S(2)}) %all-to-all-start.3) | async-done | bytes 32800 | tf_op jit(solution)/shard_map/all_to_all | solution.py:153
  151.8 3.3 all-to-all-start.1
  155.9 4.1 %all-to-all-done.1 = bf16[8,4,1,512]{3,1,2,0:T(4,128)(2,1)S(1)} async-done(((bf16[8,4,1,512]{3,1,2,0:T(4,128)(2,1)}), bf16[8,4,1,512]{3,1,2,0:T(4,128)(2,1)S(1)}, u32[]{:S(2)}, u32[]{:S(2)}) %all-to-all-start.1) | async-done | bytes 32800 | tf_op jit(solution)/shard_map/all_to_all | solution.py:153
  161.1 1.2 fusion.46
  162.9 52.6 %all-reduce.14.cloned.1.call-done = (bf16[32,1,2048]{2,0,1:T(8,128)(2,1)}, bf16[32,1,2048]{2,0,1:T(8,128)(2,1)}) async-done(((bf16[32,1,2048]{2,0,1:T(8,128)(2,1)}, bf16[32,1,2048]{2,0,1:T(8,128)(2,1)}), (bf16[32,1,2048]{2,0,1:T(8,128)(2,1)}, bf16[32,1,2048]{2,0,1:T(8,128)(2,1)})) %all-reduce.14.cloned.1.call-update) | async-done | bytes 262160
  216.3 19.0 %all-reduce.8 = (bf16[4,1,2048]{2,0,1:T(4,128)(2,1)S(1)}, bf16[4,1,2048]{2,0,1:T(4,128)(2,1)S(1)}) all-reduce(bf16[4,1,2048]{2,0,1:T(4,128)(2,1)S(1)} %get-tuple-element.37, bf16[4,1,2048]{2,0,1:T(4,128)(2,1)S(1)} %get-tuple-element.36), channel_id=1, replica_groups=mesh['req'=8,'rep'=4] {'rep'}, use_global_device_ids=true, to_apply=%region_7.8 | all-reduce | flops 16384 | bytes 65536 | tf_op jit(solution)/shard_map/psum | solution.py:62
  235.6 8.7 %all_gather.27 = bf16[32,1,2048]{2,1,0:T(2,128)(2,1)S(1)} all-gather(bf16[4,1,2048]{2,1,0:T(2,128)(2,1)S(1)} %copy.224), channel_id=1, replica_groups=mesh['req'=8,'rep'=4] {'req'}, dimensions={0}, use_global_device_ids=true | all-gather | bytes 147456 | tf_op jit(solution)/shard_map/all_gather | solution.py:183
  244.3 9.2 %all_gather.24 = bf16[32,1,2048]{2,1,0:T(2,128)(2,1)S(1)} all-gather(bf16[4,1,2048]{2,1,0:T(2,128)(2,1)S(1)} %copy.206), channel_id=1, replica_groups=mesh['req'=8,'rep'=4] {'req'}, dimensions={0}, use_global_device_ids=true | all-gather | bytes 147456 | tf_op jit(solution)/shard_map/all_gather | solution.py:183
  253.5 3.6 %fusion.8 = f32[32,1408]{1,0:T(8,128)S(1)} fusion(bf16[1,2048,1408]{2,1,0:T(8,128)(2,1)} %param.23, bf16[32,1,2048]{2,1,0:T(2,128)(2,1)S(1)} %all_gather.27), kind=kOutput, calls=%fused_computation.14 | convolution fusion | flops 184549376 | bytes 6078464 | tf_op jit(solution)/shard_map/bsd,df->bsf/dot_general | solution.py:184
  257.1 3.6 %fusion.10 = f32[32,1408]{1,0:T(8,128)S(1)} fusion(bf16[1,2048,1408]{2,1,0:T(8,128)(2,1)} %param.23, bf16[32,1,2048]{2,1,0:T(2,128)(2,1)S(1)} %all_gather.24), kind=kOutput, calls=%fused_computation.16 | convolution fusion | flops 184549376 | bytes 6078464 | tf_op jit(solution)/shard_map/bsd,df->bsf/dot_general | solution.py:184
  260.7 7.0 %fusion.51 = bf16[32,1,2048]{2,0,1:T(8,128)(2,1)} fusion(bf16[1,1408,2048]{2,1,0:T(8,128)(2,1)} %param.25, bf16[1,2048,1408]{2,1,0:T(8,128)(2,1)} %param.24, f32[32,1408]{1,0:T(8,128)S(1)} %fusion.8, f32[32]{0:T(128)S(1)} %get-tuple-element.7, bf16[32,1,2048]{2,1,0:T(2,128)(2,1)S(1)} %all_gather.27), kind=kOutput, calls=%fused_computation.43 | convolution fusion | flops 369500160 | bytes 11976832 | tf_op jit(solution)/shard_map/bsf,fd->bsd/dot_general | solution.py:192
  267.8 7.0 %fusion.48 = bf16[32,1,2048]{2,0,1:T(8,128)(2,1)} fusion(bf16[1,1408,2048]{2,1,0:T(8,128)(2,1)} %param.25, bf16[1,2048,1408]{2,1,0:T(8,128)(2,1)} %param.24, f32[32,1408]{1,0:T(8,128)S(1)} %fusion.10, f32[32]{0:T(128)S(1)} %get-tuple-element.6, bf16[32,1,2048]{2,1,0:T(2,128)(2,1)S(1)} %all_gather.24), kind=kOutput, calls=%fused_computation.42 | convolution fusion | flops 369500160 | bytes 11976832 | tf_op jit(solution)/shard_map/bsf,fd->bsd/dot_general | solution.py:192
  274.8 51.1 %all-reduce.12.cloned.1.call-done = (bf16[32,1,2048]{2,0,1:T(8,128)(2,1)}, bf16[32,1,2048]{2,0,1:T(8,128)(2,1)}) async-done(((bf16[32,1,2048]{2,0,1:T(8,128)(2,1)}, bf16[32,1,2048]{2,0,1:T(8,128)(2,1)}), (bf16[32,1,2048]{2,0,1:T(8,128)(2,1)}, bf16[32,1,2048]{2,0,1:T(8,128)(2,1)})) %all-reduce.12.cloned.1.call-update) | async-done | bytes 262160
  327.5 19.0 %all-reduce.7 = (bf16[4,1,2048]{2,0,1:T(4,128)(2,1)S(1)}, bf16[4,1,2048]{2,0,1:T(4,128)(2,1)S(1)}) all-reduce(bf16[4,1,2048]{2,0,1:T(4,128)(2,1)S(1)} %constant_dynamic-slice_fusion, bf16[4,1,2048]{2,0,1:T(4,128)(2,1)S(1)} %constant_dynamic-slice_fusion.2), channel_id=1, replica_groups=mesh['req'=8,'rep'=4] {'rep'}, use_global_device_ids=true, to_apply=%region_23.25 | all-reduce | flops 16384 | bytes 65536 | tf_op jit(solution)/shard_map/psum | solution.py:62
  (113 shorter events, 23.7 us)
Async XLA Ops:
  6.5 153.4 %copy-start = (bf16[1,512,2048]{2,1,0:T(8,128)(2,1)S(1)}, bf16[1,512,2048]{2,1,0:T(8,128)(2,1)}, u32[]{:S(2)}) copy-start(bf16[1,512,2048]{2,1,0:T(8,128)(2,1)} %param.22) | copy-start | bytes 6291460
  22.6 101.7 %all-to-all-start = ((bf16[8,4,1,512]{3,1,2,0:T(4,128)(2,1)}), bf16[8,4,1,512]{3,1,2,0:T(4,128)(2,1)S(1)}, u32[]{:S(2)}, u32[]{:S(2)}) async-start(bf16[8,4,1,512]{3,1,2,0:T(4,128)(2,1)} %bitcast.7), calls=%async_computation | async-start | bytes 65536 | tf_op jit(solution)/shard_map/all_to_all | solution.py:130
  81.1 8.4 %copy-start.6 = (s32[4]{0:T(128)S(1)}, s32[4]{0:T(128)}, u32[]{:S(2)}) copy-start(s32[4]{0:T(128)} %param.28) | copy-start | bytes 52
  81.1 8.5 %copy-start.1 = (bf16[2048,2,512]{2,1,0:T(2,128)(2,1)S(1)}, bf16[2048,2,512]{2,1,0:T(2,128)(2,1)}, u32[]{:S(2)}) copy-start(bf16[2048,2,512]{2,1,0:T(2,128)(2,1)} %param.20) | copy-start | bytes 12582916
  89.4 0.7 copy-start.5
  122.5 9.5 %copy-start.4 = (pred[2]{0:T(512)(128)(4,1)S(1)}, pred[2]{0:T(512)(128)(4,1)}, u32[]{:S(2)}) copy-start(pred[2]{0:T(512)(128)(4,1)} %constant.100) | copy-start | bytes 10
  124.4 8.5 %all-to-all-start.2 = ((bf16[8,4,1,512]{3,1,2,0:T(4,128)(2,1)}), bf16[8,4,1,512]{3,1,2,0:T(4,128)(2,1)S(1)}, u32[]{:S(2)}, u32[]{:S(2)}) async-start(bf16[8,4,1,512]{3,1,2,0:T(4,128)(2,1)} %bitcast.35), calls=%async_computation.2 | async-start | bytes 65536 | tf_op jit(solution)/shard_map/all_to_all | solution.py:130
  137.7 3.5 copy-start.2
  142.0 20.4 %copy-start.3 = (bf16[4,2,2048]{2,1,0:T(2,128)(2,1)S(1)}, bf16[4,2,2048]{2,1,0:T(2,128)(2,1)}, u32[]{:S(2)}) copy-start(bf16[4,2,2048]{2,1,0:T(2,128)(2,1)} %param.18) | copy-start | bytes 98308
  143.0 8.8 %all-to-all-start.3 = ((bf16[8,4,1,512]{3,1,2,0:T(4,128)(2,1)}), bf16[8,4,1,512]{3,1,2,0:T(4,128)(2,1)S(1)}, u32[]{:S(2)}, u32[]{:S(2)}) async-start(bf16[8,4,1,512]{3,1,2,0:T(4,128)(2,1)} %copy.223), calls=%async_computation.3 | async-start | bytes 65536 | tf_op jit(solution)/shard_map/all_to_all | solution.py:153
  151.8 8.1 %all-to-all-start.1 = ((bf16[8,4,1,512]{3,1,2,0:T(4,128)(2,1)}), bf16[8,4,1,512]{3,1,2,0:T(4,128)(2,1)S(1)}, u32[]{:S(2)}, u32[]{:S(2)}) async-start(bf16[8,4,1,512]{3,1,2,0:T(4,128)(2,1)} %copy.203), calls=%async_computation.1 | async-start | bytes 65536 | tf_op jit(solution)/shard_map/all_to_all | solution.py:153
  155.2 60.3 %all-reduce.14.cloned.1.call-start = ((), (), s32[]{:S(2)}) async-start(), calls=%async_computation.5 | async-start | bytes 524288
  162.3 163.6 %all-reduce.12.cloned.1.call-start = ((), (), s32[]{:S(2)}) async-start(), calls=%async_computation.4 | async-start | bytes 524288
Sparse Core Ops, SparseCore 0:
  162.4 53.0 all-reduce.13
  274.9 50.9 all-reduce.11
where the time goes:
time: 356 us; the launch traced here: 354 us
  waiting for transfers between devices  112 us (31%)
  blocking collectives  101 us (28%)
  local copies, waits for them, and re-layouts  63.4 us (18%)
  matrix products  43.3 us (12%)
  between operations  15 us (4%)
  starting transfers between devices  14.2 us (4%)
  other arithmetic  5.54 us (2%)
    unnamed x4, waiting for transfers between devices  104 us
    psum x2, blocking collectives, combine(): return lax.psum(partial_value, 'rep').astype(jnp.float32)  37.9 us
    gather x1, local copies, waits for them, and re-layouts, shards(): kv_pages[page_table].reshape(rows_dev, -1, 2, heads_rep, head_dim)  25.4 us
    all_gather x2, blocking collectives, section(): block_rows = lax.all_gather(hidden_normed, 'req', axis=0, tiled=True)  17.9 us
    dot_general x2, matrix products, ffn_term(): jnp.einsum('bsf,fd->bsd', hidden_units, w_down[0], preferred_element_type...  14.1 us
    reshape x1, local copies, waits for them, and re-layouts, shards(): kv_pages[page_table].reshape(rows_dev, -1, 2, heads_rep, head_dim)  14 us
    all_gather x1, blocking collectives, shards(): lax.all_gather(normed[:, 0:1], 'req', axis=0, tiled=True)  10.8 us
    all_gather x1, blocking collectives, shards(): lax.all_gather(route_ids, 'req', axis=0, tiled=True)  8.87 us
  transfers between devices with their start and end apart: 6, of which 4 were waited for; matrix products, arithmetic and copies ran while one was open for 20% of the time, Pallas kernels for 0%

commit v1 on v0

v1 whole, which is shorter than its diff:
```python
import math

import jax
import jax.numpy as jnp
from jax import lax
from jax.sharding import PartitionSpec as P

HD = 128
EXPERTS = 8
EPSILON = 1e-06
MASKED = -1e30


def normalize(values, gain_row):
    scaling = lax.rsqrt(jnp.mean(values * values, axis=-1, keepdims=True) + EPSILON)
    return (values * scaling * gain_row).astype(jnp.bfloat16)


def swap(blocks, axis):
    return lax.all_to_all(blocks, axis, split_axis=0, concat_axis=0, tiled=True)


def share_all(block, axis):
    return swap(jnp.broadcast_to(block[None], (lax.axis_size(axis),) + block.shape), axis)


def dot32(spec, left, right):
    return jnp.einsum(spec, left, right, preferred_element_type=jnp.float32)


def combine(partial):
    count = lax.axis_size("req")
    blocks = partial.astype(jnp.bfloat16).reshape((count, -1) + partial.shape[1:])
    mine = jnp.sum(swap(blocks, "req").astype(jnp.float32), axis=0).astype(jnp.bfloat16)
    return jnp.sum(share_all(mine, "rep").astype(jnp.float32), axis=0)


def pool_mask(page_table, cache_len, pages, page):
    requests, listed = page_table.shape
    start = jnp.arange(listed, dtype=jnp.int32)[None, :] * page
    count = jnp.clip(cache_len[:, None] - start, 0, page)
    owner = page_table[:, :, None] == jnp.arange(pages, dtype=jnp.int32)
    held = jnp.sum(jnp.where(owner, count[:, :, None], 0), axis=1)
    alive = jnp.arange(page, dtype=jnp.int32)[None, None, :] < held[:, :, None]
    return alive.reshape(requests, pages * page)


def attend(queries, keys, values, alive, extra_keys, extra_values):
    inv_scale = 1.0 / math.sqrt(queries.shape[-1])
    rows, steps, picks, heads, _ = queries.shape
    cache = dot32("jskhc,nhc->hjskn", queries, keys) * inv_scale
    cache = jnp.where(alive[None, :, None, None, :], cache, MASKED)
    extra = dot32("jskhc,jxhc->hjskx", queries, extra_keys) * inv_scale
    seen = jnp.arange(2)[None, :] <= jnp.arange(steps)[:, None]
    extra = jnp.where(seen[None, None, :, None, :], extra, MASKED)
    highest = jnp.maximum(jnp.max(cache, axis=-1), jnp.max(extra, axis=-1))[..., None]
    cache_exp = jnp.exp(cache - highest)
    extra_exp = jnp.exp(extra - highest)
    total = (jnp.sum(cache_exp, axis=-1) + jnp.sum(extra_exp, axis=-1))[..., None]
    cache_weight = (cache_exp / total).astype(jnp.bfloat16)
    extra_weight = (extra_exp / total).astype(jnp.bfloat16)
    mixture = dot32("hjskn,nhc->jskhc", cache_weight, values)
    mixture = mixture + dot32("hjskx,jxhc->jskhc", extra_weight, extra_values)
    return mixture.astype(jnp.bfloat16)


def shards(
    tokens,
    norm_gains,
    w_kv,
    w_query,
    w_out,
    w_gate,
    w_up,
    w_down,
    kv_pages,
    page_table,
    cache_len,
    route_ids,
    route_gates,
    new_slot,
):
    rows_dev, steps, width = tokens.shape
    count = lax.axis_size("req")
    all_rows = rows_dev * count
    holders = count // EXPERTS
    expert = lax.axis_index("req") // holders
    heads_rep = kv_pages.shape[-1] // HD
    heads_dev = w_query.shape[-1] // HD
    pages, page = kv_pages.shape[:2]
    inputs = tokens.astype(jnp.float32)
    normed = normalize(inputs, norm_gains[0])
    payload = jnp.concatenate(
        [
            normed.reshape(rows_dev, steps * width),
            route_ids.reshape(rows_dev, 8).astype(jnp.bfloat16),
            route_gates.reshape(rows_dev, 8),
            new_slot[:, None].astype(jnp.bfloat16),
            jnp.zeros((rows_dev, 111), jnp.bfloat16),
        ],
        axis=1,
    )
    got = share_all(payload, "req").reshape(all_rows, -1)
    base = steps * width
    all_normed = got[:, :base].reshape(all_rows, steps, width)
    ids = got[:, base : base + 8].astype(jnp.int32).reshape(all_rows, 2, 2, 2)
    gates = got[:, base + 8 : base + 16].astype(jnp.float32).reshape(all_rows, 2, 2, 2)
    slot = got[:, base + 16].astype(jnp.int32)
    moved = (slot[:, None] == jnp.arange(all_rows, dtype=jnp.int32)).astype(jnp.bfloat16)
    second = dot32("ib,bd->id", moved, all_normed[:, 1]).astype(jnp.bfloat16)
    rows = jnp.stack([all_normed[:, 0], second], axis=1)
    queries = dot32("bsd,dc->bsc", rows, w_query[0]).astype(jnp.bfloat16)
    arrived = swap(queries.reshape(count, rows_dev, steps, heads_dev * HD), "req")
    arrived = arrived.reshape(EXPERTS, holders, rows_dev, steps, heads_dev, HD)
    own = lax.dynamic_slice_in_dim(rows, lax.axis_index("req") * rows_dev, rows_dev, axis=0)
    fresh = dot32("jsd,dtc->jstc", own, w_kv).astype(jnp.bfloat16)
    fresh = fresh.reshape(rows_dev, 2, 2, heads_rep, HD)
    mine = new_slot[:, None] == jnp.arange(all_rows, dtype=jnp.int32)
    moved_ids = jnp.sum(jnp.where(mine[:, :, None], ids[None, :, 0, 1], 0), axis=1)
    own_ids = jnp.stack([route_ids[:, 0, 0], moved_ids], axis=1)
    chosen = (own_ids[..., None] == jnp.arange(EXPERTS, dtype=jnp.int32)).astype(jnp.bfloat16)
    picked = dot32("jske,egjshc->jskghc", chosen, arrived).astype(jnp.bfloat16)
    picked = picked.reshape(rows_dev, steps, 2, heads_rep, HD)
    keys = kv_pages[:, :, 0].reshape(pages * page, heads_rep, HD)
    values = kv_pages[:, :, 1].reshape(pages * page, heads_rep, HD)
    alive = pool_mask(page_table, cache_len, pages, page)
    result = attend(picked, keys, values, alive, fresh[:, :, 0], fresh[:, :, 1])
    result = result.reshape(rows_dev, steps, 2, holders, heads_dev, HD)
    spread = dot32("jske,jskghc->egjshc", chosen, result).astype(jnp.bfloat16)
    returned = swap(spread.reshape(count, rows_dev, steps, heads_dev * HD), "req")
    returned = returned.reshape(all_rows, steps, heads_dev * HD)
    back = dot32("ib,ic->bc", moved, returned[:, 1]).astype(jnp.bfloat16)
    answers = jnp.stack([returned[:, 0], back], axis=1)
    shares = jnp.sum(jnp.where(ids == expert, gates, 0.0), axis=-1)
    attn = dot32("bsc,cd->bsd", answers, w_out[0]) * shares[:, 0, :, None]
    hidden = inputs + combine(attn)
    hidden_normed = normalize(hidden, norm_gains[1])
    block = share_all(hidden_normed, "req").reshape(all_rows, steps, width)
    gate_part = dot32("bsd,df->bsf", block, w_gate[0])
    up_part = dot32("bsd,df->bsf", block, w_up[0])
    units = (jax.nn.silu(gate_part) * up_part).astype(jnp.bfloat16)
    feed = dot32("bsf,fd->bsd", units, w_down[0]) * shares[:, 1, :, None]
    return (hidden + combine(feed)).astype(jnp.bfloat16)


def solution(mesh):
    in_specs = (
        P("req", None, None),
        P(),
        P(None, None, "rep"),
        P("req", None, "rep"),
        P("req", "rep", None),
        P("req", None, "rep"),
        P("req", None, "rep"),
        P("req", "rep", None),
        P("req", None, None, "rep"),
        P("req", None),
        P("req"),
        P("req", None, None, None),
        P("req", None, None, None),
        P("req"),
    )
    out_specs = P("req", None, None)
    return jax.shard_map(shards, mesh=mesh, in_specs=in_specs, out_specs=out_specs, check_vma=False)
```

time: 356 us -> 164 us (0.46)
  waiting for transfers between devices: 112 us -> 9.31 us
  blocking collectives: 101 us -> 47 us
  matrix products: 43.3 us -> 23.9 us
  between operations: 15 us -> 0.33 us
    unnamed x4 -> x0, waiting for transfers between devices: 104 us -> none
    all_gather x6 -> x0, blocking collectives: 54.6 us -> none  [the longest x2 17.9 us: section(): block_rows = lax.all_gather(hidden_normed, 'req', axis=0, tiled=True)]
    all_to_all x0 -> x5, blocking collectives: none -> 47 us  [swap(): return lax.all_to_all(blocks, axis, split_axis=0, concat_axis=0, tiled=True)]
    psum x2 -> x0, blocking collectives: 37.9 us -> none  [combine(): return lax.psum(partial_value, 'rep').astype(jnp.float32)]
    slice x6 -> x7, local copies, waits for them, and re-layouts: 9.37 us -> 42.5 us  [the longest x1 41 us: shards(): keys = kv_pages[:, :, 0].reshape(pages * page, heads_rep, HD)]
    gather x5 -> x0, local copies, waits for them, and re-layouts: 27.8 us -> none  [the longest x1 25.4 us: shards(): kv_pages[page_table].reshape(rows_dev, -1, 2, heads_rep, head_dim)]
    dot_general x20 -> x13, matrix products: 43.3 us -> 23.9 us  [dot32(): return jnp.einsum(spec, left, right, preferred_element_type=jnp.float32)]
    another operation x10 -> x4, local copies, waits for them, and re-layouts: 1.62 us -> 14.6 us  [the longest x1 6.93 us: shards(): keys = kv_pages[:, :, 0].reshape(pages * page, heads_rep, HD)]
  transfers between devices with their start and end apart: 6 -> 3, of which waited for: 4 -> 2; matrix products, arithmetic and copies ran while one was open for 20% -> 35% of each run, Pallas kernels for 0% -> 0%
where the time goes in v1:
time: 164 us; the launch traced here: 163 us
  local copies, waits for them, and re-layouts  63.5 us (39%)
  blocking collectives  47 us (29%)
  matrix products  23.9 us (15%)
  starting transfers between devices  12.9 us (8%)
  waiting for transfers between devices  9.31 us (6%)
  other arithmetic  5.65 us (3%)
    all_to_all x5, blocking collectives, swap(): return lax.all_to_all(blocks, axis, split_axis=0, concat_axis=0, tiled=True)  47 us
    slice x1, local copies, waits for them, and re-layouts, shards(): keys = kv_pages[:, :, 0].reshape(pages * page, heads_rep, HD)  41 us
    dot_general x13, matrix products, dot32(): return jnp.einsum(spec, left, right, preferred_element_type=jnp.float32)  23.9 us
    all_to_all x3, starting transfers between devices, swap(): return lax.all_to_all(blocks, axis, split_axis=0, concat_axis=0, tiled=True)  12.9 us
    all_to_all x3, waiting for transfers between devices, swap(): return lax.all_to_all(blocks, axis, split_axis=0, concat_axis=0, tiled=True)  9.31 us
    another operation x1, local copies, waits for them, and re-layouts, shards(): keys = kv_pages[:, :, 0].reshape(pages * page, heads_rep, HD)  6.93 us
    another operation x1, local copies, waits for them, and re-layouts, shards(): values = kv_pages[:, :, 1].reshape(pages * page, heads_rep, HD)  6.92 us
  transfers between devices with their start and end apart: 3, of which 2 were waited for; matrix products, arithmetic and copies ran while one was open for 35% of the time, Pallas kernels for 0%

profile of v1, /device:TPU:0, one launch (start us, length us, event | category | flops | bytes accessed | tf_op | source)
XLA Modules:
  0.0 162.6 jit_solution(3308908281279972759)
XLA Ops:
  0.0 0.9 fusion.93
  0.9 0.9 fusion.61
  1.8 0.7 convert_element_type.85
  2.6 0.7 convert_bitcast_fusion
  3.3 0.8 copy.173
  4.1 0.8 fusion.63
  5.1 0.8 broadcast_in_dim.77
  5.9 5.2 %all-to-all-start = ((bf16[8,4,4224]{2,1,0:T(4,128)(2,1)}), bf16[8,4,4224]{2,1,0:T(4,128)(2,1)S(1)}, u32[]{:S(2)}, u32[]{:S(2)}) async-start(bf16[8,4,4224]{2,1,0:T(4,128)(2,1)} %broadcast_in_dim.77), calls=%async_computation | async-start | bytes 540672 | tf_op jit(solution)/shard_map/all_to_all | solution.py:20
  11.0 0.7 iota_compare_fusion.7
  11.8 41.0 %slice_reduce_fusion.1 = (bf16[256,16,512]{2,1,0:T(8,128)(2,1)}, bf16[256,16,512]{2,1,0:T(8,128)(2,1)}) fusion(bf16[256,16,2,512]{3,2,1,0:T(2,128)(2,1)} %param.22), kind=kLoop, calls=%fused_computation.1 | loop fusion | bytes 16777216 | tf_op jit(solution)/shard_map/slice | solution.py:124
  53.7 6.9 %reshape_squeeze.6 = bf16[4096,4,128]{2,1,0:T(4,128)(2,1)} reshape(bf16[256,16,512]{2,1,0:T(8,128)(2,1)} %get-tuple-element.5) | data formatting | bytes 8388608 | tf_op jit(solution)/shard_map/reshape;squeeze | solution.py:124
  60.6 6.9 %reshape_squeeze.7 = bf16[4096,4,128]{2,1,0:T(4,128)(2,1)} reshape(bf16[256,16,512]{2,1,0:T(8,128)(2,1)} %get-tuple-element.6) | data formatting | bytes 8388608 | tf_op jit(solution)/shard_map/reshape;squeeze | solution.py:125
  67.5 0.7 slice_bitcast_fusion.3
  69.5 2.9 %fusion.45 = bf16[4,2,2,512]{3,0,2,1:T(4,128)(2,1)S(1)} fusion(bf16[2048,2,512]{2,1,0:T(2,128)(2,1)} %param.16, s32[]{:T(128)S(6)} %select_n.29, bf16[32,1,2048]{2,0,1:T(8,128)(2,1)S(1)} %copy.228, bf16[32,1,2048]{2,0,1:T(8,128)(2,1)S(1)} %fusion.26), kind=kOutput, calls=%fused_computation.37 | convolution fusion | flops 33628160 | bytes 4472836 | tf_op jit(solution)/shard_map/jsd,dtc->jstc/dot_general | solution.py:28
  72.4 2.1 %fusion.30 = bf16[32,2,512]{2,0,1:T(8,128)(2,1)S(1)} fusion(bf16[1,2048,512]{2,1,0:T(8,128)(2,1)} %param.17, bf16[32,1,2048]{2,0,1:T(8,128)(2,1)S(1)} %fusion.26, bf16[32,1,2048]{2,0,1:T(8,128)(2,1)S(1)} %copy.228), kind=kOutput, calls=%fused_computation.27 | convolution fusion | flops 134381568 | bytes 2424832 | tf_op jit(solution)/shard_map/bsd,dc->bsc/dot_general | solution.py:28
  74.5 0.7 copy.215
  75.2 4.2 %all-to-all-start.1 = ((bf16[8,4,2,512]{3,2,1,0:T(2,128)(2,1)}), bf16[8,4,2,512]{3,2,1,0:T(2,128)(2,1)S(1)}, u32[]{:S(2)}, u32[]{:S(2)}) async-start(bf16[8,4,2,512]{3,2,1,0:T(2,128)(2,1)} %bitcast.14), calls=%async_computation.1 | async-start | bytes 131072 | tf_op jit(solution)/shard_map/all_to_all | solution.py:20
  79.8 4.5 %all-to-all-done.1 = bf16[8,4,2,512]{3,2,1,0:T(2,128)(2,1)S(1)} async-done(((bf16[8,4,2,512]{3,2,1,0:T(2,128)(2,1)}), bf16[8,4,2,512]{3,2,1,0:T(2,128)(2,1)S(1)}, u32[]{:S(2)}, u32[]{:S(2)}) %all-to-all-start.1) | async-done | bytes 65568 | tf_op jit(solution)/shard_map/all_to_all | solution.py:20
  85.2 3.5 %fusion.95 = (f32[4,4,2,2]{1,3,2,0:T(2,128)S(1)}, f32[4,4,2,2,4096]{4,1,3,2,0:T(4,128)S(1)}) fusion(bf16[4096,4,128,1,1]{2,1,0,4,3:T(4,128)(2,1)} %bitcast.122, bf16[4,2,2,4,128]{4,2,3,1,0:T(2,128)(2,1)S(1)} %convolution_convert_fusion.3, pred[4,4096]{1,0:T(4,128)(4,1)S(1)} %broadcast_compare_fusion), kind=kOutput, calls=%fused_computation.123 | convolution fusion | flops 67895232 | bytes 5275904 | tf_op jit(solution)/shard_map/jskhc,nhc->hjskn/dot_general | solution.py:28
  89.1 0.5 fusion.48
  89.9 3.3 %fusion.42 = bf16[4,2,2,4,128]{4,0,2,1,3:T(4,128)(2,1)S(1)} fusion(bf16[4096,4,128,1,1]{2,1,0,4,3:T(4,128)(2,1)} %bitcast.121, f32[4,4,2,2,4096]{4,1,3,2,0:T(4,128)S(1)} %get-tuple-element.22, f32[4,4,2,2]{1,3,2,0:T(2,128)S(1)} %copy.192, f32[4,4,2,2]{1,3,2,0:T(2,128)S(1)} %copy.188, f32[4,4,128,2,2]{2,4,3,1,0:T(2,128)S(1)} %fusion.76), kind=kOutput, calls=%fused_computation.36 | convolution fusion | flops 67911680 | bytes 5292544 | tf_op jit(solution)/shard_map/hjskn,nhc->jskhc/dot_general | solution.py:28
  93.5 0.7 copy.199
  94.2 3.5 %all-to-all-start.2 = ((bf16[8,4,2,512]{3,2,1,0:T(2,128)(2,1)}), bf16[8,4,2,512]{3,2,1,0:T(2,128)(2,1)S(1)}, u32[]{:S(2)}, u32[]{:S(2)}) async-start(bf16[8,4,2,512]{3,2,1,0:T(2,128)(2,1)} %copy.199), calls=%async_computation.2 | async-start | bytes 131072 | tf_op jit(solution)/shard_map/all_to_all | solution.py:20
  97.7 4.8 %all-to-all-done.2 = bf16[8,4,2,512]{3,2,1,0:T(2,128)(2,1)S(1)} async-done(((bf16[8,4,2,512]{3,2,1,0:T(2,128)(2,1)}), bf16[8,4,2,512]{3,2,1,0:T(2,128)(2,1)S(1)}, u32[]{:S(2)}, u32[]{:S(2)}) %all-to-all-start.2) | async-done | bytes 65568 | tf_op jit(solution)/shard_map/all_to_all | solution.py:20
  103.6 9.3 %all_to_all.40 = bf16[8,4,2,2048]{3,1,2,0:T(4,128)(2,1)S(1)} all-to-all(bf16[8,4,2,2048]{3,1,2,0:T(4,128)(2,1)S(1)} %copy.202), channel_id=1, replica_groups=mesh['req'=8,'rep'=4] {'req'}, dimensions={0} | all-to-all | bytes 524288 | tf_op jit(solution)/shard_map/all_to_all | solution.py:20
  113.1 10.6 %all_to_all.41 = bf16[4,4,2,2048]{3,1,2,0:T(4,128)(2,1)S(1)} all-to-all(bf16[4,4,2,2048]{3,1,2,0:T(4,128)(2,1)S(1)} %broadcast_in_dim.124), channel_id=1, replica_groups=mesh['req'=8,'rep'=4] {'rep'}, dimensions={0} | all-to-all | bytes 262144 | tf_op jit(solution)/shard_map/all_to_all | solution.py:20
  124.1 9.3 %all_to_all.42 = bf16[8,4,2,2048]{3,1,2,0:T(4,128)(2,1)S(1)} all-to-all(bf16[8,4,2,2048]{3,1,2,0:T(4,128)(2,1)S(1)} %broadcast_in_dim.125), channel_id=1, replica_groups=mesh['req'=8,'rep'=4] {'req'}, dimensions={0} | all-to-all | bytes 524288 | tf_op jit(solution)/shard_map/all_to_all | solution.py:20
  133.6 3.7 %fusion.4 = f32[32,2,1408]{2,0,1:T(8,128)S(1)} fusion(bf16[32,2,2048]{2,0,1:T(8,128)(2,1)S(1)} %reshape.197, bf16[1,2048,1408]{2,1,0:T(8,128)(2,1)} %param.19), kind=kOutput, calls=%fused_computation.6 | convolution fusion | flops 369098752 | bytes 6389760 | tf_op jit(solution)/shard_map/bsd,df->bsf/dot_general | solution.py:28
  137.3 6.4 %fusion.19 = bf16[32,2,2048]{2,0,1:T(8,128)(2,1)S(1)} fusion(bf16[1,1408,2048]{2,1,0:T(8,128)(2,1)} %param.21, bf16[32,2,2048]{2,0,1:T(8,128)(2,1)S(1)} %reshape.197, bf16[1,2048,1408]{2,1,0:T(8,128)(2,1)} %param.20, f32[32,2,1408]{2,0,1:T(8,128)S(1)} %fusion.4, f32[32,2]{0,1:T(2,128)S(1)} %get-tuple-element.17), kind=kOutput, calls=%fused_computation.19 | convolution fusion | flops 739000320 | bytes 12419328 | tf_op jit(solution)/shard_map/bsf,fd->bsd/dot_general | solution.py:28
  144.0 9.3 %all_to_all.43 = bf16[8,4,2,2048]{3,1,2,0:T(4,128)(2,1)S(1)} all-to-all(bf16[8,4,2,2048]{3,1,2,0:T(4,128)(2,1)S(1)} %copy.205), channel_id=1, replica_groups=mesh['req'=8,'rep'=4] {'req'}, dimensions={0} | all-to-all | bytes 524288 | tf_op jit(solution)/shard_map/all_to_all | solution.py:20
  153.5 8.4 %all_to_all.44 = bf16[4,4,2,2048]{3,1,2,0:T(4,128)(2,1)S(1)} all-to-all(bf16[4,4,2,2048]{3,1,2,0:T(4,128)(2,1)S(1)} %broadcast_in_dim.126), channel_id=1, replica_groups=mesh['req'=8,'rep'=4] {'rep'}, dimensions={0} | all-to-all | bytes 262144 | tf_op jit(solution)/shard_map/all_to_all | solution.py:20
  162.0 0.6 copy.207
  (77 shorter events, 6.9 us)
Async XLA Ops:
  0.0 102.8 %copy-start = (bf16[1,512,2048]{2,1,0:T(8,128)(2,1)S(1)}, bf16[1,512,2048]{2,1,0:T(8,128)(2,1)}, u32[]{:S(2)}) copy-start(bf16[1,512,2048]{2,1,0:T(8,128)(2,1)} %param.18) | copy-start | bytes 6291460
  5.9 62.4 %all-to-all-start = ((bf16[8,4,4224]{2,1,0:T(4,128)(2,1)}), bf16[8,4,4224]{2,1,0:T(4,128)(2,1)S(1)}, u32[]{:S(2)}, u32[]{:S(2)}) async-start(bf16[8,4,4224]{2,1,0:T(4,128)(2,1)} %broadcast_in_dim.77), calls=%async_computation | async-start | bytes 540672 | tf_op jit(solution)/shard_map/all_to_all | solution.py:20
  11.8 41.0 %copy-start.3 = (s32[4]{0:T(128)S(1)}, s32[4]{0:T(128)}, u32[]{:S(2)}) copy-start(s32[4]{0:T(128)} %param.24) | copy-start | bytes 52
  11.8 41.1 %copy-start.2 = (s32[4,64]{1,0:T(4,128)S(1)}, s32[4,64]{1,0:T(4,128)}, u32[]{:S(2)}) copy-start(s32[4,64]{1,0:T(4,128)} %param.23) | copy-start | bytes 3076
  75.2 9.2 %all-to-all-start.1 = ((bf16[8,4,2,512]{3,2,1,0:T(2,128)(2,1)}), bf16[8,4,2,512]{3,2,1,0:T(2,128)(2,1)S(1)}, u32[]{:S(2)}, u32[]{:S(2)}) async-start(bf16[8,4,2,512]{3,2,1,0:T(2,128)(2,1)} %bitcast.14), calls=%async_computation.1 | async-start | bytes 131072 | tf_op jit(solution)/shard_map/all_to_all | solution.py:20
  93.2 30.5 %copy-start.1 = (bf16[4,2,2048]{2,1,0:T(2,128)(2,1)S(1)}, bf16[4,2,2048]{2,1,0:T(2,128)(2,1)}, u32[]{:S(2)}) copy-start(bf16[4,2,2048]{2,1,0:T(2,128)(2,1)} %param.14) | copy-start | bytes 98308
  94.2 8.3 %all-to-all-start.2 = ((bf16[8,4,2,512]{3,2,1,0:T(2,128)(2,1)}), bf16[8,4,2,512]{3,2,1,0:T(2,128)(2,1)S(1)}, u32[]{:S(2)}, u32[]{:S(2)}) async-start(bf16[8,4,2,512]{3,2,1,0:T(2,128)(2,1)} %copy.199), calls=%async_computation.2 | async-start | bytes 131072 | tf_op jit(solution)/shard_map/all_to_all | solution.py:20

commit v2 on v1

v2 whole, which is shorter than its diff:
```python
import functools
import math

import jax
import jax.numpy as jnp
from jax import lax
from jax.experimental import pallas as pl
from jax.experimental.pallas import tpu as pltpu
from jax.sharding import PartitionSpec as P

HD = 128
EXPERTS = 8
EPSILON = 1e-06
MASKED = -1e30


def pool_mask(page_table, cache_len, pages, page):
    requests, listed = page_table.shape
    start = jnp.arange(listed, dtype=jnp.int32)[None, :] * page
    count = jnp.clip(cache_len[:, None] - start, 0, page)
    owner = page_table[:, :, None] == jnp.arange(pages, dtype=jnp.int32)
    held = jnp.sum(jnp.where(owner, count[:, :, None], 0), axis=1)
    alive = jnp.arange(page, dtype=jnp.int32)[None, None, :] < held[:, :, None]
    return alive.reshape(requests, pages * page)


CHUNK = 4096
MESH = pl.DeviceIdType.MESH


def dot32(left, right):
    return jnp.dot(left, right, preferred_element_type=jnp.float32)


def dot_rows(left, right):
    return lax.dot_general(left, right, (((1,), (1,)), ((), ())), preferred_element_type=jnp.float32)


def iota32(shape, dim):
    return lax.broadcasted_iota(jnp.int32, shape, dim).astype(jnp.float32)


def half_norm(values, gains):
    half = values.shape[0] // 2
    squares = jnp.sum(values * values, axis=-1, keepdims=True)
    mean = (squares[:half] + squares[half:]) / (2.0 * values.shape[1])
    scaling = lax.rsqrt(mean + EPSILON)
    left = jnp.broadcast_to(gains[0:1], (half, values.shape[1]))
    right = jnp.broadcast_to(gains[1:2], (half, values.shape[1]))
    gain = jnp.concatenate([left, right], axis=0)
    return (values * jnp.concatenate([scaling, scaling], axis=0) * gain).astype(jnp.bfloat16)


def whole_rows(buffer):
    count, twice, half_width = buffer.shape
    rows = twice // 2
    wide = buffer[...].astype(jnp.float32)
    left = wide[:, :rows].reshape(count * rows, half_width)
    right = wide[:, rows:].reshape(count * rows, half_width)
    return jnp.concatenate([left, right], axis=1).astype(jnp.bfloat16)


def layer_kernel(
    holders,
    tok_ref,
    gain_ref,
    meta_ref,
    bias_ref,
    kv_ref,
    wkv_ref,
    wq_ref,
    wo_ref,
    wg_ref,
    wu_ref,
    wd_ref,
    out_ref,
    kv_buf,
    wkv_buf,
    chunk_buf,
    stage,
    wq,
    wo,
    wg,
    wu,
    wd,
    act_buf,
    norm1,
    meta,
    q_send,
    q_recv,
    a_send,
    a_recv,
    p_send1,
    p_recv1,
    h_recv1,
    norm2,
    p_send2,
    p_recv2,
    h_recv2,
    weight_sem,
    chunk_sem,
    send_sem,
    recv_sem,
    rep_send_sem,
    rep_recv_sem,
):
    count = norm1.shape[0]
    reps = h_recv1.shape[0]
    rows = meta.shape[1]
    all_rows = count * rows
    half_width = norm1.shape[2]
    head_cols = wq.shape[1]
    heads = kv_buf.shape[0] // 2
    me = lax.axis_index("req")
    rep = lax.axis_index("rep")
    expert = (me // holders).astype(jnp.float32)
    pending = []

    loads = []
    for place, (source, target) in enumerate(
        ((wq_ref, wq), (wo_ref, wo), (wg_ref, wg), (wu_ref, wu), (wd_ref, wd))
    ):
        loads.append(pltpu.make_async_copy(source, target, weight_sem.at[place]))
    loads[0].start()

    barrier = pltpu.get_barrier_semaphore()
    for step in range(1, count):
        peer = lax.rem(me + step, count)
        pl.semaphore_signal(barrier, inc=1, device_id={"req": peer}, device_id_type=MESH)
    for step in range(1, reps):
        peer = lax.rem(rep + step, reps)
        pl.semaphore_signal(barrier, inc=1, device_id={"rep": peer}, device_id_type=MESH)

    def send_req(phase, block_of, target):
        copies = []
        for step in range(1, count):
            peer = lax.rem(me + step, count)
            copy = pltpu.make_async_remote_copy(
                src_ref=block_of(peer),
                dst_ref=target.at[me],
                send_sem=send_sem.at[phase, step],
                recv_sem=recv_sem.at[phase, step],
                device_id={"req": peer},
                device_id_type=MESH,
            )
            copy.start()
            copies.append(copy)
        pending.extend(copies)
        return copies

    def send_rep(phase, target):
        copies = []
        for step in range(1, reps):
            peer = lax.rem(rep + step, reps)
            copy = pltpu.make_async_remote_copy(
                src_ref=target.at[rep],
                dst_ref=target.at[rep],
                send_sem=rep_send_sem.at[phase, step],
                recv_sem=rep_recv_sem.at[phase, step],
                device_id={"rep": peer},
                device_id_type=MESH,
            )
            copy.start()
            copies.append(copy)
        pending.extend(copies)
        return copies

    def arrive(copies):
        for copy in copies:
            copy.wait_recv()

    def split_chunks(source, target, first, last):
        def fetch(index):
            return pltpu.make_async_copy(
                source.at[pl.ds(pl.multiple_of(index * CHUNK, CHUNK), CHUNK)],
                chunk_buf.at[lax.rem(index, 2)],
                chunk_sem.at[lax.rem(index, 2)],
            )

        per_chunk = CHUNK // (2 * heads)
        fetch(jnp.int32(first)).start()

        @pl.loop(first, last)
        def _(index):
            fetch(index).wait()

            @pl.when(index + 1 < last)
            def _():
                fetch(index + 1).start()

            stage[...] = chunk_buf[lax.rem(index, 2)].astype(jnp.float32)
            spot = pl.ds(pl.multiple_of(index * per_chunk, per_chunk), per_chunk)
            for part in range(2 * heads):
                target[part, spot, :] = stage[
                    pl.ds(part, per_chunk, stride=2 * heads), :
                ].astype(jnp.bfloat16)

    inputs = tok_ref[...].astype(jnp.float32)
    norm1[me] = half_norm(inputs, gain_ref[0])
    meta[me] = meta_ref[...]
    pl.semaphore_wait(barrier, count - 1 + reps - 1)
    norm_copies = send_req(0, lambda peer: norm1.at[me], norm1)
    meta_copies = send_req(1, lambda peer: meta.at[me], meta)

    kv_chunks = kv_ref.shape[0] // CHUNK
    wkv_chunks = wkv_ref.shape[0] // CHUNK
    split_chunks(kv_ref, kv_buf, 0, kv_chunks // 2)
    for load in loads[1:]:
        load.start()

    arrive(norm_copies)
    arrive(meta_copies)
    normed = whole_rows(norm1)
    table = meta[...].reshape(all_rows, 128)
    table16 = table.astype(jnp.bfloat16)
    moved = jnp.where(table[:, 0:1] == iota32((all_rows, all_rows), 1), 1.0, 0.0)
    moved = moved.astype(jnp.bfloat16)
    own_moved = jnp.where(meta_ref[:, 0:1] == iota32((rows, all_rows), 1), 1.0, 0.0)
    own_moved = own_moved.astype(jnp.bfloat16)
    pick_lane = jnp.where(iota32((8, 128), 1) == 0.0, 1.0, 0.0).astype(jnp.bfloat16)
    target_row = dot_rows(pick_lane, table16)[0:1]
    moved_back = jnp.where(target_row == iota32((all_rows, all_rows), 0), 1.0, 0.0)
    moved_back = moved_back.astype(jnp.bfloat16)

    loads[0].wait()
    queries = dot32(normed, wq[...]).astype(jnp.bfloat16)
    q_send[...] = dot32(moved, queries).reshape(count, rows, head_cols)
    q_recv[me] = q_send[me]
    q_copies = send_req(2, lambda peer: q_send.at[peer], q_recv)

    split_chunks(wkv_ref, wkv_buf, 0, wkv_chunks)
    own_rows = dot32(own_moved, normed).astype(jnp.bfloat16)
    own_table = dot32(own_moved, table16)
    for part in range(2 * heads):
        fresh = dot32(own_rows, wkv_buf[part])
        padded = jnp.concatenate([fresh, jnp.zeros((128 - rows, HD), jnp.float32)], axis=0)
        kv_buf[part, pl.ds(kv_buf.shape[1] - 128, 128), :] = padded.astype(jnp.bfloat16)
    split_chunks(kv_ref, kv_buf, kv_chunks // 2, kv_chunks)

    arrive(q_copies)
    picked = []
    for k in range(2):
        wanted = own_table[:, 1 + k : 2 + k]
        blocks = []
        for part in range(holders):
            block = jnp.zeros((rows, head_cols), jnp.float32)
            for number in range(EXPERTS):
                arrived = q_recv[number * holders + part]
                block = block + jnp.where(wanted == float(number), arrived, 0.0)
            blocks.append(block)
        picked.append(jnp.concatenate(blocks, axis=1) if holders > 1 else blocks[0])

    bias = bias_ref[...]
    bias = jnp.concatenate([bias, bias], axis=0)
    mixed = []
    for head in range(heads):
        columns = slice(head * HD, (head + 1) * HD)
        query = jnp.concatenate([picked[0][:, columns], picked[1][:, columns]], axis=0)
        scores = dot_rows(query.astype(jnp.bfloat16), kv_buf[2 * head]) * (1.0 / math.sqrt(HD))
        scores = scores + bias
        weight = jnp.exp(scores - jnp.max(scores, axis=-1, keepdims=True))
        total = jnp.sum(weight, axis=-1, keepdims=True)
        mixture = dot32(weight.astype(jnp.bfloat16), kv_buf[2 * head + 1]) / total
        mixed.append(mixture.astype(jnp.bfloat16).astype(jnp.float32))
    result = jnp.concatenate(mixed, axis=1)
    for number in range(EXPERTS):
        block = jnp.zeros((rows, heads * HD), jnp.float32)
        for k in range(2):
            wanted = own_table[:, 1 + k : 2 + k]
            part = result[k * rows : (k + 1) * rows]
            block = block + jnp.where(wanted == float(number), part, 0.0)
        for part in range(holders):
            a_send[number * holders + part] = block[:, part * head_cols : (part + 1) * head_cols]
    a_recv[me] = a_send[me]
    arrive(send_req(3, lambda peer: a_send.at[peer], a_recv))

    def share_of(router):
        share = jnp.zeros((all_rows, 1), jnp.float32)
        for k in range(2):
            number = table[:, 1 + 2 * router + k : 2 + 2 * router + k]
            gate = table[:, 5 + 2 * router + k : 6 + 2 * router + k]
            share = share + jnp.where(number == expert, gate, 0.0)
        return share

    def project(values, weights, share, blocks):
        @pl.loop(0, half_width // 256)
        def _(index):
            offset = pl.multiple_of(index * 256, 256)
            left = dot32(values, weights[:, pl.ds(offset, 256)]) * share
            right = dot32(values, weights[:, pl.ds(half_width + offset, 256)]) * share
            both = jnp.concatenate(
                [left.reshape(count, rows, 256), right.reshape(count, rows, 256)], axis=1
            )
            blocks[:, :, pl.ds(offset, 256)] = both.astype(jnp.bfloat16)

    def combine(phase, rep_phase, blocks, landed, summed):
        landed[me] = blocks[me]
        arrive(send_req(phase, lambda peer: blocks.at[peer], landed))
        summed[rep] = jnp.sum(landed[...].astype(jnp.float32), axis=0).astype(jnp.bfloat16)
        arrive(send_rep(rep_phase, summed))
        return jnp.sum(summed[...].astype(jnp.float32), axis=0)

    answers = a_recv[...].reshape(all_rows, head_cols).astype(jnp.bfloat16)
    answers = dot32(moved_back, answers).astype(jnp.bfloat16)
    loads[1].wait()
    project(answers, wo, share_of(0), p_send1)
    hidden = inputs + combine(4, 0, p_send1, p_recv1, h_recv1)
    norm2[me] = half_norm(hidden, gain_ref[1])
    arrive(send_req(5, lambda peer: norm2.at[me], norm2))
    block_rows = whole_rows(norm2)
    loads[2].wait()
    loads[3].wait()

    @pl.loop(0, wg.shape[1] // 128)
    def _(index):
        span = pl.ds(pl.multiple_of(index * 128, 128), 128)
        both = dot32(block_rows, jnp.concatenate([wg[:, span], wu[:, span]], axis=1))
        gate_part, up_part = both[:, :128], both[:, 128:]
        units = gate_part / (1.0 + jnp.exp(-gate_part)) * up_part
        act_buf[:, span] = units.astype(jnp.bfloat16)

    loads[4].wait()
    project(act_buf[...], wd, share_of(1), p_send2)
    out_ref[...] = (hidden + combine(6, 1, p_send2, p_recv2, h_recv2)).astype(jnp.bfloat16)
    for copy in pending:
        copy.wait_send()


def shards(
    tokens,
    norm_gains,
    w_kv,
    w_query,
    w_out,
    w_gate,
    w_up,
    w_down,
    kv_pages,
    page_table,
    cache_len,
    route_ids,
    route_gates,
    new_slot,
):
    rows_dev, steps, width = tokens.shape
    rows = rows_dev * steps
    half_width = width // 2
    count = lax.axis_size("req")
    reps = lax.axis_size("rep")
    holders = count // EXPERTS
    pages, page, _, kv_cols = kv_pages.shape
    heads = kv_cols // HD
    positions = pages * page
    head_cols = w_query.shape[-1]
    units = w_gate.shape[-1]
    f32, bf16 = jnp.float32, jnp.bfloat16

    def interleaved(array, length):
        return array.reshape(length, 2, heads, HD).transpose(0, 2, 1, 3).reshape(-1, HD)

    halves = tokens.reshape(rows, 2, half_width).transpose(1, 0, 2).reshape(2 * rows, half_width)
    base = (lax.axis_index("req") * rows_dev + jnp.arange(rows_dev, dtype=jnp.int32)) * steps
    target = jnp.stack([base, new_slot * steps + 1], axis=1).reshape(rows, 1)
    ids = route_ids.transpose(0, 2, 1, 3).reshape(rows, 4)
    gates = route_gates.transpose(0, 2, 1, 3).reshape(rows, 4)
    meta = jnp.concatenate(
        [target.astype(f32), ids.astype(f32), gates.astype(f32), jnp.zeros((rows, 119), f32)],
        axis=1,
    )
    alive = pool_mask(page_table, cache_len, pages, page)
    alive = jnp.repeat(alive, steps, axis=0)
    place = jnp.arange(rows)[:, None]
    extra = jnp.arange(128)[None, :]
    extra_alive = (extra // steps == place // steps) & (extra <= place)
    bias = jnp.where(jnp.concatenate([alive, extra_alive], axis=1), 0.0, MASKED)

    any_spec = pl.BlockSpec(memory_space=pl.ANY)
    vmem_spec = pl.BlockSpec(memory_space=pltpu.VMEM)
    block = (count, 2 * rows, half_width)
    rep_block = (reps, 2 * rows, half_width)
    head_block = (count, rows, head_cols)
    scratch = [
        pltpu.VMEM((2 * heads, positions + 128, HD), bf16),
        pltpu.VMEM((2 * heads, width, HD), bf16),
        pltpu.VMEM((2, CHUNK, HD), bf16),
        pltpu.VMEM((CHUNK, HD), f32),
        pltpu.VMEM((width, head_cols), bf16),
        pltpu.VMEM((head_cols, width), bf16),
        pltpu.VMEM((width, units), bf16),
        pltpu.VMEM((width, units), bf16),
        pltpu.VMEM((units, width), bf16),
        pltpu.VMEM((count * rows, units), bf16),
        pltpu.VMEM(block, bf16),
        pltpu.VMEM((count, rows, 128), f32),
        pltpu.VMEM(head_block, f32),
        pltpu.VMEM(head_block, f32),
        pltpu.VMEM(head_block, f32),
        pltpu.VMEM(head_block, f32),
        pltpu.VMEM(block, bf16),
        pltpu.VMEM(block, bf16),
        pltpu.VMEM(rep_block, bf16),
        pltpu.VMEM(block, bf16),
        pltpu.VMEM(block, bf16),
        pltpu.VMEM(block, bf16),
        pltpu.VMEM(rep_block, bf16),
        pltpu.SemaphoreType.DMA((5,)),
        pltpu.SemaphoreType.DMA((2,)),
        pltpu.SemaphoreType.DMA((7, count)),
        pltpu.SemaphoreType.DMA((7, count)),
        pltpu.SemaphoreType.DMA((2, reps)),
        pltpu.SemaphoreType.DMA((2, reps)),
    ]
    out = pl.pallas_call(
        functools.partial(layer_kernel, holders),
        out_shape=jax.ShapeDtypeStruct((2 * rows, half_width), bf16),
        in_specs=[vmem_spec] * 4 + [any_spec] * 7,
        out_specs=vmem_spec,
        scratch_shapes=scratch,
        compiler_params=pltpu.CompilerParams(
            collective_id=0, has_side_effects=True, vmem_limit_bytes=58 * 1024 * 1024
        ),
    )(
        halves,
        norm_gains.reshape(2, 2, half_width),
        meta,
        bias,
        interleaved(kv_pages, positions),
        interleaved(w_kv, width),
        w_query[0],
        w_out[0],
        w_gate[0],
        w_up[0],
        w_down[0],
    )
    out = out.reshape(2, rows, half_width).transpose(1, 0, 2)
    return out.reshape(rows_dev, steps, width)


def solution(mesh):
    in_specs = (
        P("req", None, None),
        P(),
        P(None, None, "rep"),
        P("req", None, "rep"),
        P("req", "rep", None),
        P("req", None, "rep"),
        P("req", None, "rep"),
        P("req", "rep", None),
        P("req", None, None, "rep"),
        P("req", None),
        P("req"),
        P("req", None, None, None),
        P("req", None, None, None),
        P("req"),
    )
    out_specs = P("req", None, None)
    return jax.shard_map(shards, mesh=mesh, in_specs=in_specs, out_specs=out_specs, check_vma=False)
```

time: 164 us -> 76.4 us (0.47)
  Pallas kernels: 0 us -> 64.8 us
  local copies, waits for them, and re-layouts: 63.5 us -> 5.57 us
  blocking collectives: 47 us -> 0 us
  matrix products: 23.9 us -> 0 us
  starting transfers between devices: 12.9 us -> 0 us
  waiting for transfers between devices: 9.31 us -> 0 us
    pallas_call x0 -> x1, Pallas kernels: none -> 64.8 us  [shards(): pl.pallas_call(functools.partial(layer_kernel, holders), out_shape=jax.Sh...]
    all_to_all x5 -> x0, blocking collectives: 47 us -> none  [swap(): return lax.all_to_all(blocks, axis, split_axis=0, concat_axis=0, tiled=True)]
    slice x7 -> x0, local copies, waits for them, and re-layouts: 42.5 us -> none  [the longest x1 41 us: shards(): keys = kv_pages[:, :, 0].reshape(pages * page, heads_rep, HD)]
    dot_general x13 -> x0, matrix products: 23.9 us -> none  [dot32(): return jnp.einsum(spec, left, right, preferred_element_type=jnp.float32)]
    another operation x4 -> x0, local copies, waits for them, and re-layouts: 14.6 us -> none  [the longest x1 6.93 us: shards(): keys = kv_pages[:, :, 0].reshape(pages * page, heads_rep, HD)]
    all_to_all x3 -> x0, starting transfers between devices: 12.9 us -> none  [swap(): return lax.all_to_all(blocks, axis, split_axis=0, concat_axis=0, tiled=True)]
    all_to_all x3 -> x0, waiting for transfers between devices: 9.31 us -> none  [swap(): return lax.all_to_all(blocks, axis, split_axis=0, concat_axis=0, tiled=True)]
    reduce_sum x10 -> x0, other arithmetic: 2.12 us -> none  [the longest x2 0.98 us: normalize(): jnp.mean(values * values, axis=-1, keepdims=True) + EPSILON]
  transfers between devices with their start and end apart: 3 -> 0, of which waited for: 2 -> 0; matrix products, arithmetic and copies ran while one was open for 35% -> 0% of each run, Pallas kernels for 0% -> 0%
where the time goes in v2:
time: 76.4 us; the launch traced here: 75.5 us
  Pallas kernels  64.8 us (85%)
  local copies, waits for them, and re-layouts  5.57 us (7%)
  other arithmetic  5.03 us (7%)
    pallas_call x1, Pallas kernels, shards(): pl.pallas_call(functools.partial(layer_kernel, holders), out_shape=jax.Sh...  64.8 us

profile of v2, /device:TPU:0, one launch (start us, length us, event | category | flops | bytes accessed | tf_op | source)
XLA Modules:
  0.0 75.5 jit_solution(1547712692390124123)
XLA Ops:
  0.0 0.7 subtract_clamp_fusion
  0.7 0.8 %select_reduce_fusion = s32[4,256]{1,0:T(4,128)S(1)} fusion(s32[4,64]{1,0:T(4,128)S(1)} %subtract_clamp_fusion, s32[4,64]{1,0:T(4,128)} %param.23), kind=kLoop, calls=%fused_computation | loop fusion | flops 195584 | bytes 6144 | tf_op jit(solution)/shard_map/reduce_sum | solution.py:22
  1.6 0.2 lt.23
  1.8 0.3 lt.24
  2.1 0.1 lt.21
  2.2 0.1 broadcast_in_dim.38
  2.3 0.1 reshape.175
  2.4 0.1 fusion
  2.5 0.7 add_select_fusion.bias_ref
  3.1 0.8 %reshape.172 = bf16[8,2,1024]{2,1,0:T(2,128)(2,1)S(1)} reshape(bf16[4,2,2048]{2,1,0:T(2,128)(2,1)} %param.14) | data formatting | bytes 65536 | tf_op jit(solution)/shard_map/reshape | solution.py:361
  3.9 0.6 copy.50
  4.5 0.7 convert_bitcast_fusion.1
  5.2 0.1 copy.45
  5.3 0.1 reshape.183
  5.4 0.7 convert_bitcast_fusion
  6.1 0.1 copy.46
  6.2 0.1 reshape.184
  6.3 0.7 add_bitcast_fusion
  7.0 0.1 copy.36
  7.1 0.1 convert_element_type.42
  7.2 0.1 pad.5.clone
  7.2 0.7 maximum_maximum_fusion.meta_ref
  7.9 1.3 %reshape.174.gain_ref = f32[2,2,1024]{2,1,0:T(2,128)} reshape(f32[2,2048]{1,0:T(2,128)} %param.15) | data formatting | bytes 32768 | tf_op jit(solution)/shard_map/reshape | solution.py:424
  9.2 64.8 %shard_map.136 = bf16[16,1024]{1,0:T(8,128)(2,1)} custom-call(bf16[16,1024]{1,0:T(8,128)(2,1)} %bitcast.36, f32[2,2,1024]{2,1,0:T(2,128)} %reshape.174.gain_ref, f32[8,128]{1,0:T(8,128)} %maximum_maximum_fusion.meta_ref, f32[8,4224]{1,0:T(8,128)} %add_select_fusion.bias_ref, bf16[32768,128]{1,0:T(8,128)(2,1)} %bitcast.29, bf16[16384,128]{1,0:T(8,128)(2,1)} %bitcast.33, ...), custom_call_target="tpu_custom_call" | custom-call | tf_op jit(solution)/shard_map/pallas_call | solution.py:413
  74.1 0.8 %copy.44 = bf16[8,2,1024]{2,1,0:T(2,128)(2,1)S(1)} copy(bf16[8,2,1024]{2,0,1:T(8,128)(2,1)} %bitcast.37) | data formatting | bytes 65536 | tf_op jit(solution)/shard_map/transpose | solution.py:435
  74.9 0.6 reshape.181
  (8 shorter events, 0.1 us)

commit v3 on v2

--- a/solution.py
+++ b/solution.py
@@ -14,16 +14,6 @@
 MASKED = -1e30
 
 
-def pool_mask(page_table, cache_len, pages, page):
-    requests, listed = page_table.shape
-    start = jnp.arange(listed, dtype=jnp.int32)[None, :] * page
-    count = jnp.clip(cache_len[:, None] - start, 0, page)
-    owner = page_table[:, :, None] == jnp.arange(pages, dtype=jnp.int32)
-    held = jnp.sum(jnp.where(owner, count[:, :, None], 0), axis=1)
-    alive = jnp.arange(page, dtype=jnp.int32)[None, None, :] < held[:, :, None]
-    return alive.reshape(requests, pages * page)
-
-
 CHUNK = 4096
 MESH = pl.DeviceIdType.MESH
 
@@ -45,8 +35,9 @@
     squares = jnp.sum(values * values, axis=-1, keepdims=True)
     mean = (squares[:half] + squares[half:]) / (2.0 * values.shape[1])
     scaling = lax.rsqrt(mean + EPSILON)
-    left = jnp.broadcast_to(gains[0:1], (half, values.shape[1]))
-    right = jnp.broadcast_to(gains[1:2], (half, values.shape[1]))
+    width = values.shape[1]
+    left = jnp.broadcast_to(gains[:, :width], (half, width))
+    right = jnp.broadcast_to(gains[:, width:], (half, width))
     gain = jnp.concatenate([left, right], axis=0)
     return (values * jnp.concatenate([scaling, scaling], axis=0) * gain).astype(jnp.bfloat16)
 
@@ -64,8 +55,11 @@
     holders,
     tok_ref,
     gain_ref,
-    meta_ref,
-    bias_ref,
+    ids_ref,
+    gates_ref,
+    slot_ref,
+    table_ref,
+    length_ref,
     kv_ref,
     wkv_ref,
     wq_ref,
@@ -76,8 +70,10 @@
     out_ref,
     kv_buf,
     wkv_buf,
-    chunk_buf,
-    stage,
+    kv_raw,
+    wkv_raw,
+    tok_buf,
+    bias_buf,
     wq,
     wo,
     wg,
@@ -98,7 +94,8 @@
     p_recv2,
     h_recv2,
     weight_sem,
-    chunk_sem,
+    kv_sem,
+    wkv_sem,
     send_sem,
     recv_sem,
     rep_send_sem,
@@ -122,6 +119,17 @@
     ):
         loads.append(pltpu.make_async_copy(source, target, weight_sem.at[place]))
     loads[0].start()
+    kv_loads = []
+    wkv_loads = []
+    for source, target, sems, chunk_loads in (
+        (kv_ref, kv_raw, kv_sem, kv_loads),
+        (wkv_ref, wkv_raw, wkv_sem, wkv_loads),
+    ):
+        for index in range(source.shape[0] // CHUNK):
+            part = pl.ds(index * CHUNK, CHUNK)
+            load = pltpu.make_async_copy(source.at[part], target.at[part], sems.at[index])
+            load.start()
+            chunk_loads.append(load)
 
     barrier = pltpu.get_barrier_semaphore()
     for step in range(1, count):
@@ -169,44 +177,92 @@
         for copy in copies:
             copy.wait_recv()
 
-    def split_chunks(source, target, first, last):
-        def fetch(index):
-            return pltpu.make_async_copy(
-                source.at[pl.ds(pl.multiple_of(index * CHUNK, CHUNK), CHUNK)],
-                chunk_buf.at[lax.rem(index, 2)],
-                chunk_sem.at[lax.rem(index, 2)],
-            )
-
+    spread_rows = 256
+    per_piece = spread_rows // (2 * heads)
+    line = lax.broadcasted_iota(jnp.int32, (spread_rows, spread_rows), 0)
+    source_line = lax.rem(line, per_piece) * (2 * heads) + line // per_piece
+    column = lax.broadcasted_iota(jnp.int32, (spread_rows, spread_rows), 1)
+    sorter = jnp.where(source_line == column, 1.0, 0.0).astype(jnp.bfloat16)
+
+    def split_chunk(raw, target, load, index):
+        load.wait()
+        pieces = [
+            raw[pl.ds(index * CHUNK + spot * spread_rows, spread_rows), :]
+            for spot in range(CHUNK // spread_rows)
+        ]
+        sorted_rows = dot32(sorter, jnp.concatenate(pieces, axis=1)).astype(jnp.bfloat16)
         per_chunk = CHUNK // (2 * heads)
-        fetch(jnp.int32(first)).start()
-
-        @pl.loop(first, last)
-        def _(index):
-            fetch(index).wait()
-
-            @pl.when(index + 1 < last)
-            def _():
-                fetch(index + 1).start()
-
-            stage[...] = chunk_buf[lax.rem(index, 2)].astype(jnp.float32)
-            spot = pl.ds(pl.multiple_of(index * per_chunk, per_chunk), per_chunk)
-            for part in range(2 * heads):
-                target[part, spot, :] = stage[
-                    pl.ds(part, per_chunk, stride=2 * heads), :
-                ].astype(jnp.bfloat16)
-
-    inputs = tok_ref[...].astype(jnp.float32)
-    norm1[me] = half_norm(inputs, gain_ref[0])
-    meta[me] = meta_ref[...]
+        for part in range(2 * heads):
+            block = sorted_rows[part * per_piece : (part + 1) * per_piece]
+            for spot in range(CHUNK // spread_rows):
+                start = index * per_chunk + spot * per_piece
+                target[part, pl.ds(start, per_piece), :] = block[:, spot * HD : (spot + 1) * HD]
+
+    def split_chunks(raw, target, chunk_loads, first, last):
+        for index in range(first, last):
+            split_chunk(raw, target, chunk_loads[index], index)
+
+    for j in range(tok_ref.shape[0]):
+        both = tok_ref[j].astype(jnp.float32)
+        tok_buf[2 * j : 2 * j + 2, :] = both[:, :half_width]
+        tok_buf[rows + 2 * j : rows + 2 * j + 2, :] = both[:, half_width:]
+    inputs = tok_buf[...]
+    norm1[me] = half_norm(inputs, gain_ref[0:1, :])
+
+    line = lax.broadcasted_iota(jnp.int32, (rows, 128), 0)
+    lane = lax.broadcasted_iota(jnp.int32, (rows, 128), 1)
+    place = line * 128 + lane
+    own = me * rows + line
+    own_meta = jnp.where(lane == 0, own.astype(jnp.float32), 0.0)
+    for j in range(rows // 2):
+        moved_to = (slot_ref[j] * 2 + 1).astype(jnp.float32)
+        own_meta = jnp.where(place == (2 * j + 1) * 128, moved_to, own_meta)
+    for router in range(2):
+        for step in range(2):
+            numbers = ids_ref[router, step].astype(jnp.float32)
+            weights = gates_ref[router, step].astype(jnp.float32)
+            for k in range(2):
+                for j in range(rows // 2):
+                    spot = (2 * j + step) * 128 + 1 + 2 * router + k
+                    number = numbers[k : k + 1, j : j + 1]
+                    own_meta = jnp.where(place == spot, number, own_meta)
+                    weight = weights[k : k + 1, j : j + 1]
+                    own_meta = jnp.where(place == spot + 4, weight, own_meta)
+    meta[me] = own_meta
     pl.semaphore_wait(barrier, count - 1 + reps - 1)
     norm_copies = send_req(0, lambda peer: norm1.at[me], norm1)
     meta_copies = send_req(1, lambda peer: meta.at[me], meta)
+    for load in loads[1:]:
+        load.start()
 
     kv_chunks = kv_ref.shape[0] // CHUNK
     wkv_chunks = wkv_ref.shape[0] // CHUNK
-    split_chunks(kv_ref, kv_buf, 0, kv_chunks // 2)
-    for load in loads[1:]:
-        load.start()
+    pages = table_ref.shape[0] * table_ref.shape[1]
+    page = (kv_buf.shape[1] - 128) // pages
+    page_line = lax.broadcasted_iota(jnp.int32, (rows, pages), 0) // 2
+    page_lane = lax.broadcasted_iota(jnp.int32, (rows, pages), 1)
+
+    def place_page(index, held):
+        for j in range(rows // 2):
+            valid = jnp.clip(length_ref[j] - index * page, 0, page)
+            here = (page_lane == table_ref[j, index]) & (page_line == j)
+            held = jnp.where(here, valid, held)
+        return held
+
+    held = jnp.zeros((rows, pages), jnp.int32)
+    held = lax.fori_loop(0, table_ref.shape[1], place_page, held)
+    held = held.astype(jnp.float32).astype(jnp.bfloat16)
+    span = 512
+    span_line = lax.broadcasted_iota(jnp.int32, (pages, span), 0)
+    span_page = lax.broadcasted_iota(jnp.int32, (pages, span), 1) // page
+    within = lax.rem(lax.broadcasted_iota(jnp.int32, (rows, span), 1), page).astype(jnp.float32)
+    for index in range(pages * page // span):
+        widen = jnp.where(span_line == span_page + index * (span // page), 1.0, 0.0)
+        wide = dot32(held, widen.astype(jnp.bfloat16))
+        bias_buf[:, index * span : (index + 1) * span] = jnp.where(within < wide, 0.0, MASKED)
+    extra_alive = (lane // 2 == line // 2) & (lane <= line)
+    bias_buf[:, pages * page :] = jnp.where(extra_alive, 0.0, MASKED)
+    split_chunks(kv_raw, kv_buf, kv_loads, 0, kv_chunks // 2)
 
     arrive(norm_copies)
     arrive(meta_copies)
@@ -215,7 +271,7 @@
     table16 = table.astype(jnp.bfloat16)
     moved = jnp.where(table[:, 0:1] == iota32((all_rows, all_rows), 1), 1.0, 0.0)
     moved = moved.astype(jnp.bfloat16)
-    own_moved = jnp.where(meta_ref[:, 0:1] == iota32((rows, all_rows), 1), 1.0, 0.0)
+    own_moved = jnp.where(own_meta[:, 0:1] == iota32((rows, all_rows), 1), 1.0, 0.0)
     own_moved = own_moved.astype(jnp.bfloat16)
     pick_lane = jnp.where(iota32((8, 128), 1) == 0.0, 1.0, 0.0).astype(jnp.bfloat16)
     target_row = dot_rows(pick_lane, table16)[0:1]
@@ -228,14 +284,14 @@
     q_recv[me] = q_send[me]
     q_copies = send_req(2, lambda peer: q_send.at[peer], q_recv)
 
-    split_chunks(wkv_ref, wkv_buf, 0, wkv_chunks)
+    split_chunks(wkv_raw, wkv_buf, wkv_loads, 0, wkv_chunks)
     own_rows = dot32(own_moved, normed).astype(jnp.bfloat16)
     own_table = dot32(own_moved, table16)
     for part in range(2 * heads):
         fresh = dot32(own_rows, wkv_buf[part])
         padded = jnp.concatenate([fresh, jnp.zeros((128 - rows, HD), jnp.float32)], axis=0)
         kv_buf[part, pl.ds(kv_buf.shape[1] - 128, 128), :] = padded.astype(jnp.bfloat16)
-    split_chunks(kv_ref, kv_buf, kv_chunks // 2, kv_chunks)
+    split_chunks(kv_raw, kv_buf, kv_loads, kv_chunks // 2, kv_chunks)
 
     arrive(q_copies)
     picked = []
@@ -250,7 +306,7 @@
             blocks.append(block)
         picked.append(jnp.concatenate(blocks, axis=1) if holders > 1 else blocks[0])
 
-    bias = bias_ref[...]
+    bias = bias_buf[...]
     bias = jnp.concatenate([bias, bias], axis=0)
     mixed = []
     for head in range(heads):
@@ -305,7 +361,7 @@
     loads[1].wait()
     project(answers, wo, share_of(0), p_send1)
     hidden = inputs + combine(4, 0, p_send1, p_recv1, h_recv1)
-    norm2[me] = half_norm(hidden, gain_ref[1])
+    norm2[me] = half_norm(hidden, gain_ref[1:2, :])
     arrive(send_req(5, lambda peer: norm2.at[me], norm2))
     block_rows = whole_rows(norm2)
     loads[2].wait()
@@ -321,7 +377,11 @@
 
     loads[4].wait()
     project(act_buf[...], wd, share_of(1), p_send2)
-    out_ref[...] = (hidden + combine(6, 1, p_send2, p_recv2, h_recv2)).astype(jnp.bfloat16)
+    final = hidden + combine(6, 1, p_send2, p_recv2, h_recv2)
+    for j in range(out_ref.shape[0]):
+        left = final[2 * j : 2 * j + 2]
+        right = final[rows + 2 * j : rows + 2 * j + 2]
+        out_ref[j] = jnp.concatenate([left, right], axis=1).astype(jnp.bfloat16)
     for copy in pending:
         copy.wait_send()
 
@@ -358,32 +418,19 @@
     def interleaved(array, length):
         return array.reshape(length, 2, heads, HD).transpose(0, 2, 1, 3).reshape(-1, HD)
 
-    halves = tokens.reshape(rows, 2, half_width).transpose(1, 0, 2).reshape(2 * rows, half_width)
-    base = (lax.axis_index("req") * rows_dev + jnp.arange(rows_dev, dtype=jnp.int32)) * steps
-    target = jnp.stack([base, new_slot * steps + 1], axis=1).reshape(rows, 1)
-    ids = route_ids.transpose(0, 2, 1, 3).reshape(rows, 4)
-    gates = route_gates.transpose(0, 2, 1, 3).reshape(rows, 4)
-    meta = jnp.concatenate(
-        [target.astype(f32), ids.astype(f32), gates.astype(f32), jnp.zeros((rows, 119), f32)],
-        axis=1,
-    )
-    alive = pool_mask(page_table, cache_len, pages, page)
-    alive = jnp.repeat(alive, steps, axis=0)
-    place = jnp.arange(rows)[:, None]
-    extra = jnp.arange(128)[None, :]
-    extra_alive = (extra // steps == place // steps) & (extra <= place)
-    bias = jnp.where(jnp.concatenate([alive, extra_alive], axis=1), 0.0, MASKED)
-
     any_spec = pl.BlockSpec(memory_space=pl.ANY)
     vmem_spec = pl.BlockSpec(memory_space=pltpu.VMEM)
+    smem_spec = pl.BlockSpec(memory_space=pltpu.SMEM)
     block = (count, 2 * rows, half_width)
     rep_block = (reps, 2 * rows, half_width)
     head_block = (count, rows, head_cols)
     scratch = [
         pltpu.VMEM((2 * heads, positions + 128, HD), bf16),
         pltpu.VMEM((2 * heads, width, HD), bf16),
-        pltpu.VMEM((2, CHUNK, HD), bf16),
-        pltpu.VMEM((CHUNK, HD), f32),
+        pltpu.VMEM((positions * 2 * heads, HD), bf16),
+        pltpu.VMEM((width * 2 * heads, HD), bf16),
+        pltpu.VMEM((2 * rows, half_width), f32),
+        pltpu.VMEM((rows, positions + 128), f32),
         pltpu.VMEM((width, head_cols), bf16),
         pltpu.VMEM((head_cols, width), bf16),
         pltpu.VMEM((width, units), bf16),
@@ -404,7 +451,8 @@
         pltpu.VMEM(block, bf16),
         pltpu.VMEM(rep_block, bf16),
         pltpu.SemaphoreType.DMA((5,)),
-        pltpu.SemaphoreType.DMA((2,)),
+        pltpu.SemaphoreType.DMA((positions * 2 * heads // CHUNK,)),
+        pltpu.SemaphoreType.DMA((width * 2 * heads // CHUNK,)),
         pltpu.SemaphoreType.DMA((7, count)),
         pltpu.SemaphoreType.DMA((7, count)),
         pltpu.SemaphoreType.DMA((2, reps)),
@@ -412,18 +460,21 @@
     ]
     out = pl.pallas_call(
         functools.partial(layer_kernel, holders),
-        out_shape=jax.ShapeDtypeStruct((2 * rows, half_width), bf16),
-        in_specs=[vmem_spec] * 4 + [any_spec] * 7,
+        out_shape=jax.ShapeDtypeStruct((rows_dev, steps, width), bf16),
+        in_specs=[vmem_spec] * 4 + [smem_spec] * 3 + [any_spec] * 7,
         out_specs=vmem_spec,
         scratch_shapes=scratch,
         compiler_params=pltpu.CompilerParams(
             collective_id=0, has_side_effects=True, vmem_limit_bytes=58 * 1024 * 1024
         ),
     )(
-        halves,
-        norm_gains.reshape(2, 2, half_width),
-        meta,
-        bias,
+        tokens,
+        norm_gains,
+        route_ids.transpose(1, 2, 3, 0),
+        route_gates.transpose(1, 2, 3, 0),
+        new_slot,
+        page_table,
+        cache_len,
         interleaved(kv_pages, positions),
         interleaved(w_kv, width),
         w_query[0],
@@ -432,8 +483,7 @@
         w_up[0],
         w_down[0],
     )
-    out = out.reshape(2, rows, half_width).transpose(1, 0, 2)
-    return out.reshape(rows_dev, steps, width)
+    return out
 
 
 def solution(mesh):

time: 76.4 us -> 55.7 us (0.73)
  Pallas kernels: 64.8 us -> 54.1 us
  other arithmetic: 5.03 us -> 0 us
  local copies, waits for them, and re-layouts: 5.57 us -> 1.4 us
    pallas_call x1, Pallas kernels: 64.8 us -> 54.1 us  [shards(): pl.pallas_call(functools.partial(layer_kernel, holders), out_shape=jax.Sh...]
    reshape x5 -> x0, local copies, waits for them, and re-layouts: 3.48 us -> none  [the longest x2 1.41 us: shards(): tokens.reshape(rows, 2, half_width).transpose(1, 0, 2)]
    unnamed x0 -> x1, local copies, waits for them, and re-layouts: none -> 1.4 us
    convert_element_type x3 -> x0, other arithmetic: 1.38 us -> none  [the longest x1 0.69 us: shards(): ids.astype(f32)]
    reduce_sum x1 -> x0, other arithmetic: 0.83 us -> none  [pool_mask(): held = jnp.sum(jnp.where(owner, count[:, :, None], 0), axis=1)]
    transpose x1 -> x0, local copies, waits for them, and re-layouts: 0.79 us -> none  [shards(): out = out.reshape(2, rows, half_width).transpose(1, 0, 2)]
where the time goes in v3:
time: 55.7 us; the launch traced here: 55.5 us
  Pallas kernels  54.1 us (97%)
  local copies, waits for them, and re-layouts  1.4 us (3%)
    pallas_call x1, Pallas kernels, shards(): pl.pallas_call(functools.partial(layer_kernel, holders), out_shape=jax.Sh...  54.1 us
    unnamed x1, local copies, waits for them, and re-layouts  1.4 us

profile of v3, /device:TPU:0, one launch (start us, length us, event | category | flops | bytes accessed | tf_op | source)
XLA Modules:
  0.0 55.5 jit_solution(11115303327515842300)
XLA Ops:
  0.0 54.1 %shard_map.136 = bf16[4,2,2048]{2,1,0:T(2,128)(2,1)} custom-call(bf16[4,2,2048]{2,1,0:T(2,128)(2,1)} %tok_ref.1, f32[2,2048]{1,0:T(2,128)} %gain_ref.1, s32[2,2,2,4]{3,2,1,0:T(2,128)} %bitcast.24, bf16[2,2,2,4]{3,2,1,0:T(2,128)(2,1)} %bitcast.25, s32[4]{0:T(128)} %slot_ref.1, s32[4,64]{1,0:T(4,128)} %table_ref.1, s32[4]{0:T(128)} %length_ref.1, ...), custom_call_target="tpu_custom_call" | custom-call | tf_op jit(solution)/shard_map/pallas_call | solution.py:461
  54.1 1.4 %copy.18 = bf16[4,2,2048]{2,1,0:T(2,128)(2,1)} copy(bf16[4,2,2048]{2,1,0:T(2,128)(2,1)} %shard_map.136) | data formatting | bytes 65536

commit v4 on v3

--- a/solution.py
+++ b/solution.py
@@ -15,6 +15,7 @@
 
 
 CHUNK = 4096
+COLUMN_PARTS = 2
 MESH = pl.DeviceIdType.MESH
 
 
@@ -49,6 +50,10 @@
     left = wide[:, :rows].reshape(count * rows, half_width)
     right = wide[:, rows:].reshape(count * rows, half_width)
     return jnp.concatenate([left, right], axis=1).astype(jnp.bfloat16)
+
+
+def block_at(blocks, part, peer):
+    return blocks.at[part, peer]
 
 
 def layer_kernel(
@@ -69,7 +74,6 @@
     wd_ref,
     out_ref,
     kv_buf,
-    wkv_buf,
     kv_raw,
     wkv_raw,
     tok_buf,
@@ -102,7 +106,7 @@
     rep_recv_sem,
 ):
     count = norm1.shape[0]
-    reps = h_recv1.shape[0]
+    reps = h_recv1.shape[1]
     rows = meta.shape[1]
     all_rows = count * rows
     half_width = norm1.shape[2]
@@ -236,7 +240,6 @@
         load.start()
 
     kv_chunks = kv_ref.shape[0] // CHUNK
-    wkv_chunks = wkv_ref.shape[0] // CHUNK
     pages = table_ref.shape[0] * table_ref.shape[1]
     page = (kv_buf.shape[1] - 128) // pages
     page_line = lax.broadcasted_iota(jnp.int32, (rows, pages), 0) // 2
@@ -284,11 +287,27 @@
     q_recv[me] = q_send[me]
     q_copies = send_req(2, lambda peer: q_send.at[peer], q_recv)
 
-    split_chunks(wkv_raw, wkv_buf, wkv_loads, 0, wkv_chunks)
-    own_rows = dot32(own_moved, normed).astype(jnp.bfloat16)
+    own_rows = dot32(own_moved, normed)
     own_table = dot32(own_moved, table16)
-    for part in range(2 * heads):
-        fresh = dot32(own_rows, wkv_buf[part])
+    parts = 2 * heads
+    tile_cols = 128 * parts
+    tiles = own_rows.shape[1] // 128
+    stacked = jnp.concatenate([own_rows[:, t * 128 : (t + 1) * 128] for t in range(tiles)], axis=0)
+    repeat_line = lax.broadcasted_iota(jnp.int32, (128, tile_cols), 0)
+    repeat_lane = lax.broadcasted_iota(jnp.int32, (128, tile_cols), 1) // parts
+    repeater = jnp.where(repeat_line == repeat_lane, 1.0, 0.0).astype(jnp.bfloat16)
+    repeated = dot32(stacked.astype(jnp.bfloat16), repeater)
+    part_lane = lax.rem(lax.broadcasted_iota(jnp.int32, (rows, tile_cols), 1), parts)
+    for load in wkv_loads:
+        load.wait()
+    fresh_all = jnp.zeros((parts * rows, HD), jnp.float32)
+    for t in range(tiles):
+        tile = repeated[t * rows : (t + 1) * rows]
+        spread = [jnp.where(part_lane == part, tile, 0.0) for part in range(parts)]
+        spread = jnp.concatenate(spread, axis=0).astype(jnp.bfloat16)
+        fresh_all = fresh_all + dot32(spread, wkv_raw[t * tile_cols : (t + 1) * tile_cols, :])
+    for part in range(parts):
+        fresh = fresh_all[part * rows : (part + 1) * rows]
         padded = jnp.concatenate([fresh, jnp.zeros((128 - rows, HD), jnp.float32)], axis=0)
         kv_buf[part, pl.ds(kv_buf.shape[1] - 128, 128), :] = padded.astype(jnp.bfloat16)
     split_chunks(kv_raw, kv_buf, kv_loads, kv_chunks // 2, kv_chunks)
@@ -338,31 +357,49 @@
             share = share + jnp.where(number == expert, gate, 0.0)
         return share
 
-    def project(values, weights, share, blocks):
-        @pl.loop(0, half_width // 256)
+    def project(values, weights, share, blocks, part):
+        part_width = blocks.shape[3]
+
+        @pl.loop(0, part_width // 256)
         def _(index):
             offset = pl.multiple_of(index * 256, 256)
-            left = dot32(values, weights[:, pl.ds(offset, 256)]) * share
-            right = dot32(values, weights[:, pl.ds(half_width + offset, 256)]) * share
+            start = part * part_width + offset
+            left = dot32(values, weights[:, pl.ds(start, 256)]) * share
+            right = dot32(values, weights[:, pl.ds(half_width + start, 256)]) * share
             both = jnp.concatenate(
                 [left.reshape(count, rows, 256), right.reshape(count, rows, 256)], axis=1
             )
-            blocks[:, :, pl.ds(offset, 256)] = both.astype(jnp.bfloat16)
-
-    def combine(phase, rep_phase, blocks, landed, summed):
-        landed[me] = blocks[me]
-        arrive(send_req(phase, lambda peer: blocks.at[peer], landed))
-        summed[rep] = jnp.sum(landed[...].astype(jnp.float32), axis=0).astype(jnp.bfloat16)
-        arrive(send_rep(rep_phase, summed))
-        return jnp.sum(summed[...].astype(jnp.float32), axis=0)
+            blocks[part, :, :, pl.ds(offset, 256)] = both.astype(jnp.bfloat16)
+
+    def project_combine(values, weights, share, buffers, phase, rep_phase):
+        blocks, landed, summed = buffers
+        parts = range(blocks.shape[0])
+        req_copies, rep_copies, totals = [], [], []
+        for part in parts:
+            project(values, weights, share, blocks, part)
+            landed[part, me] = blocks[part, me]
+            copies = send_req(
+                phase + part, functools.partial(block_at, blocks, part), landed.at[part]
+            )
+            req_copies.append(copies)
+        for part in parts:
+            arrive(req_copies[part])
+            total = jnp.sum(landed[part].astype(jnp.float32), axis=0)
+            summed[part, rep] = total.astype(jnp.bfloat16)
+            rep_copies.append(send_rep(rep_phase + part, summed.at[part]))
+        for part in parts:
+            arrive(rep_copies[part])
+            totals.append(jnp.sum(summed[part].astype(jnp.float32), axis=0))
+        return jnp.concatenate(totals, axis=1)
 
     answers = a_recv[...].reshape(all_rows, head_cols).astype(jnp.bfloat16)
     answers = dot32(moved_back, answers).astype(jnp.bfloat16)
     loads[1].wait()
-    project(answers, wo, share_of(0), p_send1)
-    hidden = inputs + combine(4, 0, p_send1, p_recv1, h_recv1)
+    hidden = inputs + project_combine(
+        answers, wo, share_of(0), (p_send1, p_recv1, h_recv1), 4, 0
+    )
     norm2[me] = half_norm(hidden, gain_ref[1:2, :])
-    arrive(send_req(5, lambda peer: norm2.at[me], norm2))
+    arrive(send_req(4 + COLUMN_PARTS, lambda peer: norm2.at[me], norm2))
     block_rows = whole_rows(norm2)
     loads[2].wait()
     loads[3].wait()
@@ -376,12 +413,18 @@
         act_buf[:, span] = units.astype(jnp.bfloat16)
 
     loads[4].wait()
-    project(act_buf[...], wd, share_of(1), p_send2)
-    final = hidden + combine(6, 1, p_send2, p_recv2, h_recv2)
+    final = hidden + project_combine(
+        act_buf[...],
+        wd,
+        share_of(1),
+        (p_send2, p_recv2, h_recv2),
+        5 + COLUMN_PARTS,
+        COLUMN_PARTS,
+    )
     for j in range(out_ref.shape[0]):
         left = final[2 * j : 2 * j + 2]
         right = final[rows + 2 * j : rows + 2 * j + 2]
-        out_ref[j] = jnp.concatenate([left, right], axis=1).astype(jnp.bfloat16)
+        out_ref[j] = jnp.concatenate([left, right], axis=1)
     for copy in pending:
         copy.wait_send()
 
@@ -422,11 +465,11 @@
     vmem_spec = pl.BlockSpec(memory_space=pltpu.VMEM)
     smem_spec = pl.BlockSpec(memory_space=pltpu.SMEM)
     block = (count, 2 * rows, half_width)
-    rep_block = (reps, 2 * rows, half_width)
+    part_block = (COLUMN_PARTS, count, 2 * rows, half_width // COLUMN_PARTS)
+    rep_block = (COLUMN_PARTS, reps, 2 * rows, half_width // COLUMN_PARTS)
     head_block = (count, rows, head_cols)
     scratch = [
         pltpu.VMEM((2 * heads, positions + 128, HD), bf16),
-        pltpu.VMEM((2 * heads, width, HD), bf16),
         pltpu.VMEM((positions * 2 * heads, HD), bf16),
         pltpu.VMEM((width * 2 * heads, HD), bf16),
         pltpu.VMEM((2 * rows, half_width), f32),
@@ -443,24 +486,24 @@
         pltpu.VMEM(head_block, f32),
         pltpu.VMEM(head_block, f32),
         pltpu.VMEM(head_block, f32),
-        pltpu.VMEM(block, bf16),
-        pltpu.VMEM(block, bf16),
+        pltpu.VMEM(part_block, bf16),
+        pltpu.VMEM(part_block, bf16),
         pltpu.VMEM(rep_block, bf16),
         pltpu.VMEM(block, bf16),
-        pltpu.VMEM(block, bf16),
-        pltpu.VMEM(block, bf16),
+        pltpu.VMEM(part_block, bf16),
+        pltpu.VMEM(part_block, bf16),
         pltpu.VMEM(rep_block, bf16),
         pltpu.SemaphoreType.DMA((5,)),
         pltpu.SemaphoreType.DMA((positions * 2 * heads // CHUNK,)),
         pltpu.SemaphoreType.DMA((width * 2 * heads // CHUNK,)),
-        pltpu.SemaphoreType.DMA((7, count)),
-        pltpu.SemaphoreType.DMA((7, count)),
-        pltpu.SemaphoreType.DMA((2, reps)),
-        pltpu.SemaphoreType.DMA((2, reps)),
+        pltpu.SemaphoreType.DMA((5 + 2 * COLUMN_PARTS, count)),
+        pltpu.SemaphoreType.DMA((5 + 2 * COLUMN_PARTS, count)),
+        pltpu.SemaphoreType.DMA((2 * COLUMN_PARTS, reps)),
+        pltpu.SemaphoreType.DMA((2 * COLUMN_PARTS, reps)),
     ]
     out = pl.pallas_call(
         functools.partial(layer_kernel, holders),
-        out_shape=jax.ShapeDtypeStruct((rows_dev, steps, width), bf16),
+        out_shape=jax.ShapeDtypeStruct((rows_dev, steps, width), f32),
         in_specs=[vmem_spec] * 4 + [smem_spec] * 3 + [any_spec] * 7,
         out_specs=vmem_spec,
         scratch_shapes=scratch,
@@ -483,7 +526,7 @@
         w_up[0],
         w_down[0],
     )
-    return out
+    return out.astype(bf16)
 
 
 def solution(mesh):

time: 55.7 us -> 53.6 us (0.962)
  Pallas kernels: 54.1 us -> 51.9 us
  other arithmetic: 0 us -> 1.48 us
  local copies, waits for them, and re-layouts: 1.4 us -> 0 us
    pallas_call x1, Pallas kernels: 54.1 us -> 51.9 us  [shards(): pl.pallas_call(functools.partial(layer_kernel, holders), out_shape=jax.Sh...]
    convert_element_type x0 -> x1, other arithmetic: none -> 1.48 us  [shards(): return out.astype(bf16)]
    unnamed x1 -> x0, local copies, waits for them, and re-layouts: 1.4 us -> none
where the time goes in v4:
time: 53.6 us; the launch traced here: 53.4 us
  Pallas kernels  51.9 us (97%)
  other arithmetic  1.48 us (3%)
    pallas_call x1, Pallas kernels, shards(): pl.pallas_call(functools.partial(layer_kernel, holders), out_shape=jax.Sh...  51.9 us
    convert_element_type x1, other arithmetic, shards(): return out.astype(bf16)  1.48 us

profile of v4, /device:TPU:0, one launch (start us, length us, event | category | flops | bytes accessed | tf_op | source)
XLA Modules:
  0.0 53.4 jit_solution(8357523655208060190)
XLA Ops:
  0.0 51.9 %shard_map.136 = f32[4,2,2048]{2,1,0:T(2,128)} custom-call(bf16[4,2,2048]{2,1,0:T(2,128)(2,1)} %tok_ref.1, f32[2,2048]{1,0:T(2,128)} %gain_ref.1, s32[2,2,2,4]{3,2,1,0:T(2,128)} %bitcast.24, bf16[2,2,2,4]{3,2,1,0:T(2,128)(2,1)} %bitcast.25, s32[4]{0:T(128)} %slot_ref.1, s32[4,64]{1,0:T(4,128)} %table_ref.1, s32[4]{0:T(128)} %length_ref.1, ...), custom_call_target="tpu_custom_call" | custom-call | tf_op jit(solution)/shard_map/pallas_call | solution.py:504
  51.9 1.5 %convert_element_type.3 = bf16[4,2,2048]{2,1,0:T(2,128)(2,1)} convert(f32[4,2,2048]{2,1,0:T(2,128)} %shard_map.136) | non-fusion elementwise | flops 16384 | bytes 98304 | tf_op jit(solution)/shard_map/convert_element_type | solution.py:529

commit v5 on v4

--- a/solution.py
+++ b/solution.py
@@ -190,17 +190,18 @@
 
     def split_chunk(raw, target, load, index):
         load.wait()
-        pieces = [
-            raw[pl.ds(index * CHUNK + spot * spread_rows, spread_rows), :]
-            for spot in range(CHUNK // spread_rows)
-        ]
-        sorted_rows = dot32(sorter, jnp.concatenate(pieces, axis=1)).astype(jnp.bfloat16)
         per_chunk = CHUNK // (2 * heads)
-        for part in range(2 * heads):
-            block = sorted_rows[part * per_piece : (part + 1) * per_piece]
-            for spot in range(CHUNK // spread_rows):
-                start = index * per_chunk + spot * per_piece
-                target[part, pl.ds(start, per_piece), :] = block[:, spot * HD : (spot + 1) * HD]
+        for pair in range(CHUNK // (2 * spread_rows)):
+            pieces = [
+                raw[pl.ds(index * CHUNK + (2 * pair + side) * spread_rows, spread_rows), :]
+                for side in range(2)
+            ]
+            sorted_rows = dot32(sorter, jnp.concatenate(pieces, axis=1)).astype(jnp.bfloat16)
+            for part in range(2 * heads):
+                block = sorted_rows[part * per_piece : (part + 1) * per_piece]
+                for side in range(2):
+                    start = index * per_chunk + (2 * pair + side) * per_piece
+                    target[part, pl.ds(start, per_piece), :] = block[:, side * HD : (side + 1) * HD]
 
     def split_chunks(raw, target, chunk_loads, first, last):
         for index in range(first, last):
@@ -327,12 +328,15 @@
 
     bias = bias_buf[...]
     bias = jnp.concatenate([bias, bias], axis=0)
-    mixed = []
+    all_scores = []
     for head in range(heads):
         columns = slice(head * HD, (head + 1) * HD)
         query = jnp.concatenate([picked[0][:, columns], picked[1][:, columns]], axis=0)
         scores = dot_rows(query.astype(jnp.bfloat16), kv_buf[2 * head]) * (1.0 / math.sqrt(HD))
-        scores = scores + bias
+        all_scores.append(scores + bias)
+    mixed = []
+    for head in range(heads):
+        scores = all_scores[head]
         weight = jnp.exp(scores - jnp.max(scores, axis=-1, keepdims=True))
         total = jnp.sum(weight, axis=-1, keepdims=True)
         mixture = dot32(weight.astype(jnp.bfloat16), kv_buf[2 * head + 1]) / total

time: 53.6 us -> 52.7 us (0.983)
  Pallas kernels: 51.9 us -> 51 us
    pallas_call x1, Pallas kernels: 51.9 us -> 51 us  [shards(): pl.pallas_call(functools.partial(layer_kernel, holders), out_shape=jax.Sh...]
where the time goes in v5:
time: 52.7 us; the launch traced here: 52.5 us
  Pallas kernels  51 us (97%)
  other arithmetic  1.48 us (3%)
    pallas_call x1, Pallas kernels, shards(): pl.pallas_call(functools.partial(layer_kernel, holders), out_shape=jax.Sh...  51 us
    convert_element_type x1, other arithmetic, shards(): return out.astype(bf16)  1.48 us

profile of v5, /device:TPU:0, one launch (start us, length us, event | category | flops | bytes accessed | tf_op | source)
XLA Modules:
  0.0 52.5 jit_solution(10892385883240758464)
XLA Ops:
  0.0 51.0 %shard_map.136 = f32[4,2,2048]{2,1,0:T(2,128)} custom-call(bf16[4,2,2048]{2,1,0:T(2,128)(2,1)} %tok_ref.1, f32[2,2048]{1,0:T(2,128)} %gain_ref.1, s32[2,2,2,4]{3,2,1,0:T(2,128)} %bitcast.24, bf16[2,2,2,4]{3,2,1,0:T(2,128)(2,1)} %bitcast.25, s32[4]{0:T(128)} %slot_ref.1, s32[4,64]{1,0:T(4,128)} %table_ref.1, s32[4]{0:T(128)} %length_ref.1, ...), custom_call_target="tpu_custom_call" | custom-call | tf_op jit(solution)/shard_map/pallas_call | solution.py:508
  51.0 1.5 %convert_element_type.3 = bf16[4,2,2048]{2,1,0:T(2,128)(2,1)} convert(f32[4,2,2048]{2,1,0:T(2,128)} %shard_map.136) | non-fusion elementwise | flops 16384 | bytes 98304 | tf_op jit(solution)/shard_map/convert_element_type | solution.py:533
